TPU v7x, 128 devices: a whole 4x4x4 slice. The times are simulated.
128 devices in a mesh: segment: 16 (over z_lo, x, core), dp: 8 (over y, z_hi).
Axes of the slice: x: 4, y: 4, z: 4 (z_hi: 2, z_lo: 2; z = z_hi * 2 + z_lo), core: 2. Of those that a mesh axis runs over, the one named last changes fastest.
Arguments:
- stream_in: bfloat16 [1024, 8192], P('dp'), may hold values from -6 to 6
- sec_gain: float32 [16, 8192], P('segment'), may hold values from 0.25 to 1.75
- sec_mix: float32 [16, 8192], P('segment'), may hold values from -3 to 3
- fc_weight: bfloat16 [3, 8192, 8192], P(None, 'dp', 'segment'), may hold values from -0.0390625 to 0.0390625
- decay: float32 [8192], P('segment'), may hold values from 0.2 to 0.97
- lengths: int32 [8, 8], P('dp'), may hold values from 1 to 16
- ttt_mask: int32 [7, 1024], P(None, 'dp'), may hold values 0 or 1
Outputs:
- step_loss: float32 [8, 7], P('dp')
- fc_grad: float32 [3, 8192, 8192], P(None, 'dp', 'segment')
All inputs are finite; a program needn't handle non-finite values. No bound on the sum of `ttt_mask` on one device may be relied on, other than what follows from the above.
Results may differ from a plain program's by a relative error of at most 0.0047.
Values may be sent and summed in bfloat16 or wider, within the bound.
A program may use at most 128 MiB of HBM per device.

v0:
```python
import jax
import jax.numpy as jnp
from jax import lax
from jax.sharding import PartitionSpec as P

D = 8192
MB = 16
NMB = 8
STEPS = 7


def shifted(value, axis, steps):
    count = lax.axis_size(axis)
    first, last = (max(0, -steps), min(count, count - steps))
    return lax.ppermute(value, axis, [(source, source + steps) for source in range(first, last)])


def from_root(value, axis, root):
    mine = lax.axis_index(axis) == root
    return lax.psum(jnp.where(mine, value, jnp.zeros_like(value)), axis)


def section_step(hidden, gain, mix):
    values = hidden.astype(jnp.float32)
    scale = jnp.sqrt(jnp.mean(values * values, axis=-1, keepdims=True) + 1e-05)
    return (values + mix * jax.nn.silu(gain * values / scale)).astype(jnp.bfloat16)


def unroll_losses(joined, upper, decay, tok_len, masks, width):
    count_tok = joined.shape[0]
    columns = joined.shape[1]
    position = jnp.arange(count_tok, dtype=jnp.int32) % MB
    keep_prev = (position >= 1).astype(jnp.float32)[:, None]
    state = joined
    losses = []
    for step in range(1, STEPS + 1):
        before = jnp.concatenate([jnp.zeros((1, columns), jnp.float32), state[:-1]], 0) * keep_prev
        state = joined + decay[None, :] * masks[step - 1].astype(jnp.float32)[:, None] * before
        target = jnp.concatenate([upper[step:], jnp.zeros((step, columns), jnp.float32)], 0)
        weight = (position + step < tok_len).astype(jnp.float32)
        count = jnp.sum(weight)
        differ = state - target
        total = jnp.sum(weight[:, None] * differ * differ)
        losses.append(total / (width * jnp.maximum(count, 1.0)))
    return jnp.stack(losses)


def local(stream_in, sec_gain, sec_mix, fc_weight, decay, lengths, ttt_mask):
    segments = lax.axis_size("segment")
    segment_index = lax.axis_index("segment")
    tok_count = stream_in.shape[0]
    micro_rows = stream_in.reshape(NMB, MB, D)
    gain = sec_gain[0]
    mix = sec_mix[0]
    ticks = segments + NMB - 1
    middle_section = segments // 2
    high_section = segments - 1

    def entering(tick_index, incoming):
        first_rows = lax.dynamic_index_in_dim(
            micro_rows, jnp.clip(tick_index, 0, NMB - 1), 0, keepdims=False
        )
        return jnp.where(segment_index == 0, first_rows, incoming)

    def slot_of(tick_index):
        micro_index = tick_index - segment_index
        active = jnp.logical_and(micro_index >= 0, micro_index < NMB)
        return (active, jnp.clip(micro_index, 0, NMB - 1))

    def tick_three(tick_index, carry):
        incoming, outputs = carry
        active, slot = slot_of(tick_index)
        result = section_step(entering(tick_index, incoming), gain, mix)
        previous = lax.dynamic_index_in_dim(outputs, slot, 0, keepdims=False)
        outputs = lax.dynamic_update_index_in_dim(
            outputs, jnp.where(active, result, previous), slot, 0
        )
        incoming = shifted(result, "segment", 1)
        return (incoming, outputs)

    start_three = (jnp.zeros((MB, D), jnp.bfloat16), jnp.zeros((NMB, MB, D), jnp.bfloat16))
    _, outputs = lax.fori_loop(0, ticks, tick_three, start_three)
    low_tap = from_root(outputs, "segment", 0)
    mid_tap = from_root(outputs, "segment", middle_section)
    high_tap = from_root(outputs, "segment", high_section)
    taps = jnp.stack([low_tap, mid_tap, high_tap]).reshape(3, tok_count, D)
    features = lax.all_to_all(taps, "dp", split_axis=2, concat_axis=1, tiled=True)
    block = features
    joined = lax.psum_scatter(
        jnp.einsum("bcr,brd->cd", block, fc_weight, preferred_element_type=jnp.float32),
        "dp",
        scatter_dimension=0,
        tiled=True,
    )
    out_cols = fc_weight.shape[2]
    upper = lax.dynamic_slice_in_dim(taps[2], segment_index * out_cols, out_cols, 1).astype(
        jnp.float32
    )
    tok_len = jnp.repeat(lengths[0], MB)

    def local_objective(joined_local):
        partial_losses = unroll_losses(joined_local, upper, decay, tok_len, ttt_mask, D)
        return (jnp.sum(partial_losses), partial_losses)

    total, vjp_fn, partial_losses = jax.vjp(local_objective, joined, has_aux=True)
    joined_grad = vjp_fn(jnp.ones_like(total))[0]
    step_loss = lax.psum(partial_losses, "segment")
    grad_rows = joined_grad.astype(jnp.bfloat16)
    empty = jnp.zeros((3, fc_weight.shape[1], out_cols), jnp.float32)
    piece = jax.tree.map(lambda part: lax.all_gather(part, "dp", axis=0, tiled=True), grad_rows)
    block = lax.slice_in_dim(features, 0, piece.shape[0], axis=1)
    fc_grad = empty + jnp.einsum("bcr,cd->brd", block, piece, preferred_element_type=jnp.float32)
    return (step_loss[None, :], fc_grad)


def solution(mesh):
    in_specs = (
        P("dp", None),
        P("segment", None),
        P("segment", None),
        P(None, "dp", "segment"),
        P("segment"),
        P("dp", None),
        P(None, "dp"),
    )
    out_specs = (P("dp", None), P(None, "dp", "segment"))
    return jax.shard_map(local, mesh=mesh, in_specs=in_specs, out_specs=out_specs, check_vma=False)
```

profile of v0, /device:TPU:1, one launch (start us, length us, event | category | flops | bytes accessed | tf_op | source)
XLA Modules:
  0.0 777.5 jit_solution(4152637728945975278)
XLA Ops:
  8.8 313.5 %while.16 = (s32[]{:T(128)}, bf16[16,8192]{1,0:T(8,128)(2,1)S(1)}, bf16[8,16,8192]{2,1,0:T(8,128)(2,1)}, pred[]{:T(512)}, bf16[8,16,8192]{2,1,0:T(8,128)(2,1)}, ...) while((s32[]{:T(128)}, bf16[16,8192]{1,0:T(8,128)(2,1)S(1)}, ...), condition=%wide.region_2.3_spmd, body=%wide.region_0.2_spmd.sunk | while | flops 2097178 | bytes 3474432 | solution.py:82
  13.9 4.5 collective-permute-start
  18.4 3.6 collective-permute-done
  26.9 4.3 collective-permute-start
  31.2 3.6 collective-permute-done
  39.8 4.3 collective-permute-start
  44.1 3.6 collective-permute-done
  52.6 4.3 collective-permute-start
  56.9 3.6 collective-permute-done
  65.5 4.3 collective-permute-start
  69.8 3.6 collective-permute-done
  78.4 4.3 collective-permute-start
  82.6 3.6 collective-permute-done
  91.2 4.3 collective-permute-start
  95.5 3.6 collective-permute-done
  104.1 4.3 collective-permute-start
  108.3 3.6 collective-permute-done
  116.9 4.3 collective-permute-start
  121.2 3.6 collective-permute-done
  129.8 4.3 collective-permute-start
  134.0 3.6 collective-permute-done
  142.6 4.3 collective-permute-start
  146.9 3.6 collective-permute-done
  155.5 4.3 collective-permute-start
  168.3 4.3 collective-permute-start
  181.2 4.3 collective-permute-start
  194.0 5.0 collective-permute-start
  207.6 6.4 collective-permute-start
  222.5 6.4 collective-permute-start
  237.5 6.4 collective-permute-start
  252.5 6.4 collective-permute-start
  267.4 6.4 collective-permute-start
  273.8 3.6 collective-permute-done
  282.4 6.4 collective-permute-start
  288.8 3.6 collective-permute-done
  297.4 6.4 collective-permute-start
  312.3 6.4 collective-permute-start
  322.3 4.4 broadcast_select_fusion.2
  326.8 166.9 %all-reduce.24.cloned.1.call-done = (bf16[8,16,8192]{2,1,0:T(8,128)(2,1)}, bf16[1,128,8192]{2,1,0:T(8,128)(2,1)}, bf16[1,128,8192]{2,1,0:T(8,128)(2,1)}) async-done(((bf16[8,16,8192]{2,1,0:T(8,128)(2,1)}, bf16[1,128,8192]{2,1,0:T(8,128)(2,1)}, bf16[1,128,8192]{2,1,0:T(8,128)(2,1)}), (bf16[8,16,8192]{2,1,0:T(8,128)(2,1)}, bf16[1,128,8192]{2,1,0:T(8,128)(2,1)}, ...) | async-done | bytes 6291472 | tf_op jit(solution)/shard_map/psum | solution.py:20
  493.7 6.4 pad_maximum_fusion
  500.1 13.1 %copy.18 = bf16[3,128,8192]{1,0,2:T(4,128)(2,1)} copy(bf16[3,128,8192]{2,1,0:T(8,128)(2,1)} %pad_maximum_fusion) | data formatting | bytes 12582912 | tf_op jit(solution)/shard_map/stack | solution.py:86
  513.2 99.6 %all_to_all.18 = bf16[3,128,8192]{1,0,2:T(4,128)(2,1)S(1)} all-to-all(bf16[3,128,8192]{1,0,2:T(4,128)(2,1)} %copy.18), channel_id=1, replica_groups=mesh['segment'=16,'dp'=8] {'dp'}, dimensions={2} | all-to-all | bytes 12582912 | tf_op jit(solution)/shard_map/all_to_all | solution.py:87
  616.4 8.7 %copy.20 = bf16[3,8,128,1024]{3,2,1,0:T(8,128)(2,1)} copy(bf16[3,8,128,1024]{2,3,1,0:T(8,128)(2,1)} %bitcast.72) | data formatting | bytes 12582912 | tf_op jit(solution)/shard_map/all_to_all | solution.py:87
  625.1 7.5 convolution_bitcast_fusion
  640.8 64.8 %reduce-scatter.2.cloned.1.call-done = f32[128,512]{1,0:T(8,128)} async-done(((f32[1024,512]{1,0:T(8,128)}), f32[128,512]{1,0:T(8,128)}) %reduce-scatter.2.cloned.1.call-update) | async-done | bytes 262160 | tf_op jit(solution)/shard_map/reduce_scatter | solution.py:89
  720.3 29.6 %psum.31 = f32[1,7]{1,0:T(1,128)} all-reduce(f32[1,7]{1,0:T(1,128)S(1)} %bitcast.91), channel_id=1, replica_groups=mesh['segment'=16,'dp'=8] {'segment'}, use_global_device_ids=true, to_apply=%region_21.22 | all-reduce | flops 7 | bytes 56 | tf_op jit(solution)/shard_map/psum | solution.py:107
  749.9 11.8 %all-gather.2.cloned.1.call-done = bf16[1024,512]{1,0:T(8,128)(2,1)} async-done(((bf16[128,512]{1,0:T(8,128)(2,1)}), bf16[1024,512]{1,0:T(8,128)(2,1)}) %all-gather.2.cloned.1.call-update) | async-done | bytes 1048592 | tf_op jit(solution)/shard_map/all_gather | solution.py:110
  761.6 9.4 %fusion.3 = f32[3,1024,512]{2,1,0:T(8,128)} fusion(bf16[3,1024,1024]{2,1,0:T(8,128)(2,1)} %bitcast.77, bf16[1024,512]{1,0:T(8,128)(2,1)} %all-gather.2.cloned.1.call-done), kind=kOutput, calls=%fused_computation.16 | convolution fusion | flops 3221225472 | bytes 13631488 | tf_op jit(solution)/shard_map/bcr,cd->brd/dot_general | solution.py:112
  (166 shorter events, 169.1 us)
Async XLA Ops:
  7.2 617.9 %copy-start = (bf16[3,1024,512]{2,1,0:T(8,128)(2,1)S(1)}, bf16[3,1024,512]{2,1,0:T(8,128)(2,1)}, u32[]{:S(2)}) copy-start(bf16[3,1024,512]{2,1,0:T(8,128)(2,1)} %param.12) | copy-start | bytes 9437188
  7.2 1.6 copy-start.4
  7.2 1.6 copy-start.5
  7.2 486.5 %all-reduce.24.cloned.1.call-start = ((), (), s32[]{:S(2)}) async-start(), calls=%async_computation.4 | async-start | bytes 12582912 | tf_op jit(solution)/shard_map/psum | solution.py:20
  13.9 8.1 %collective-permute-start = (bf16[16,8192]{1,0:T(8,128)(2,1)}, bf16[16,8192]{1,0:T(8,128)(2,1)S(1)}, u32[]{:S(2)}, u32[]{:S(2)}) collective-permute-start(bf16[16,8192]{1,0:T(8,128)(2,1)} %get-tuple-element.278), channel_id=1, source_target_pairs={{0,8},{8,16},{16,24},{24,32},{32,40},{40,48},{48,56},{56,64},{64,7... | collective-permute-start | bytes 786440 | tf_op jit(solution)/shard_map/while/body/eval_jaxpr/ppermute | solution.py:15
  26.9 7.9 %collective-permute-start = (bf16[16,8192]{1,0:T(8,128)(2,1)}, bf16[16,8192]{1,0:T(8,128)(2,1)S(1)}, u32[]{:S(2)}, u32[]{:S(2)}) collective-permute-start(bf16[16,8192]{1,0:T(8,128)(2,1)} %get-tuple-element.278), channel_id=1, source_target_pairs={{0,8},{8,16},{16,24},{24,32},{32,40},{40,48},{48,56},{56,64},{64,7... | collective-permute-start | bytes 786440 | tf_op jit(solution)/shard_map/while/body/eval_jaxpr/ppermute | solution.py:15
  39.8 7.9 %collective-permute-start = (bf16[16,8192]{1,0:T(8,128)(2,1)}, bf16[16,8192]{1,0:T(8,128)(2,1)S(1)}, u32[]{:S(2)}, u32[]{:S(2)}) collective-permute-start(bf16[16,8192]{1,0:T(8,128)(2,1)} %get-tuple-element.278), channel_id=1, source_target_pairs={{0,8},{8,16},{16,24},{24,32},{32,40},{40,48},{48,56},{56,64},{64,7... | collective-permute-start | bytes 786440 | tf_op jit(solution)/shard_map/while/body/eval_jaxpr/ppermute | solution.py:15
  52.6 7.9 %collective-permute-start = (bf16[16,8192]{1,0:T(8,128)(2,1)}, bf16[16,8192]{1,0:T(8,128)(2,1)S(1)}, u32[]{:S(2)}, u32[]{:S(2)}) collective-permute-start(bf16[16,8192]{1,0:T(8,128)(2,1)} %get-tuple-element.278), channel_id=1, source_target_pairs={{0,8},{8,16},{16,24},{24,32},{32,40},{40,48},{48,56},{56,64},{64,7... | collective-permute-start | bytes 786440 | tf_op jit(solution)/shard_map/while/body/eval_jaxpr/ppermute | solution.py:15
  65.5 7.9 %collective-permute-start = (bf16[16,8192]{1,0:T(8,128)(2,1)}, bf16[16,8192]{1,0:T(8,128)(2,1)S(1)}, u32[]{:S(2)}, u32[]{:S(2)}) collective-permute-start(bf16[16,8192]{1,0:T(8,128)(2,1)} %get-tuple-element.278), channel_id=1, source_target_pairs={{0,8},{8,16},{16,24},{24,32},{32,40},{40,48},{48,56},{56,64},{64,7... | collective-permute-start | bytes 786440 | tf_op jit(solution)/shard_map/while/body/eval_jaxpr/ppermute | solution.py:15
  78.4 7.9 %collective-permute-start = (bf16[16,8192]{1,0:T(8,128)(2,1)}, bf16[16,8192]{1,0:T(8,128)(2,1)S(1)}, u32[]{:S(2)}, u32[]{:S(2)}) collective-permute-start(bf16[16,8192]{1,0:T(8,128)(2,1)} %get-tuple-element.278), channel_id=1, source_target_pairs={{0,8},{8,16},{16,24},{24,32},{32,40},{40,48},{48,56},{56,64},{64,7... | collective-permute-start | bytes 786440 | tf_op jit(solution)/shard_map/while/body/eval_jaxpr/ppermute | solution.py:15
  91.2 7.9 %collective-permute-start = (bf16[16,8192]{1,0:T(8,128)(2,1)}, bf16[16,8192]{1,0:T(8,128)(2,1)S(1)}, u32[]{:S(2)}, u32[]{:S(2)}) collective-permute-start(bf16[16,8192]{1,0:T(8,128)(2,1)} %get-tuple-element.278), channel_id=1, source_target_pairs={{0,8},{8,16},{16,24},{24,32},{32,40},{40,48},{48,56},{56,64},{64,7... | collective-permute-start | bytes 786440 | tf_op jit(solution)/shard_map/while/body/eval_jaxpr/ppermute | solution.py:15
  104.1 7.9 %collective-permute-start = (bf16[16,8192]{1,0:T(8,128)(2,1)}, bf16[16,8192]{1,0:T(8,128)(2,1)S(1)}, u32[]{:S(2)}, u32[]{:S(2)}) collective-permute-start(bf16[16,8192]{1,0:T(8,128)(2,1)} %get-tuple-element.278), channel_id=1, source_target_pairs={{0,8},{8,16},{16,24},{24,32},{32,40},{40,48},{48,56},{56,64},{64,7... | collective-permute-start | bytes 786440 | tf_op jit(solution)/shard_map/while/body/eval_jaxpr/ppermute | solution.py:15
  116.9 7.9 %collective-permute-start = (bf16[16,8192]{1,0:T(8,128)(2,1)}, bf16[16,8192]{1,0:T(8,128)(2,1)S(1)}, u32[]{:S(2)}, u32[]{:S(2)}) collective-permute-start(bf16[16,8192]{1,0:T(8,128)(2,1)} %get-tuple-element.278), channel_id=1, source_target_pairs={{0,8},{8,16},{16,24},{24,32},{32,40},{40,48},{48,56},{56,64},{64,7... | collective-permute-start | bytes 786440 | tf_op jit(solution)/shard_map/while/body/eval_jaxpr/ppermute | solution.py:15
  129.8 7.9 %collective-permute-start = (bf16[16,8192]{1,0:T(8,128)(2,1)}, bf16[16,8192]{1,0:T(8,128)(2,1)S(1)}, u32[]{:S(2)}, u32[]{:S(2)}) collective-permute-start(bf16[16,8192]{1,0:T(8,128)(2,1)} %get-tuple-element.278), channel_id=1, source_target_pairs={{0,8},{8,16},{16,24},{24,32},{32,40},{40,48},{48,56},{56,64},{64,7... | collective-permute-start | bytes 786440 | tf_op jit(solution)/shard_map/while/body/eval_jaxpr/ppermute | solution.py:15
  142.6 7.9 %collective-permute-start = (bf16[16,8192]{1,0:T(8,128)(2,1)}, bf16[16,8192]{1,0:T(8,128)(2,1)S(1)}, u32[]{:S(2)}, u32[]{:S(2)}) collective-permute-start(bf16[16,8192]{1,0:T(8,128)(2,1)} %get-tuple-element.278), channel_id=1, source_target_pairs={{0,8},{8,16},{16,24},{24,32},{32,40},{40,48},{48,56},{56,64},{64,7... | collective-permute-start | bytes 786440 | tf_op jit(solution)/shard_map/while/body/eval_jaxpr/ppermute | solution.py:15
  155.5 7.9 %collective-permute-start = (bf16[16,8192]{1,0:T(8,128)(2,1)}, bf16[16,8192]{1,0:T(8,128)(2,1)S(1)}, u32[]{:S(2)}, u32[]{:S(2)}) collective-permute-start(bf16[16,8192]{1,0:T(8,128)(2,1)} %get-tuple-element.278), channel_id=1, source_target_pairs={{0,8},{8,16},{16,24},{24,32},{32,40},{40,48},{48,56},{56,64},{64,7... | collective-permute-start | bytes 786440 | tf_op jit(solution)/shard_map/while/body/eval_jaxpr/ppermute | solution.py:15
  168.3 7.9 %collective-permute-start = (bf16[16,8192]{1,0:T(8,128)(2,1)}, bf16[16,8192]{1,0:T(8,128)(2,1)S(1)}, u32[]{:S(2)}, u32[]{:S(2)}) collective-permute-start(bf16[16,8192]{1,0:T(8,128)(2,1)} %get-tuple-element.278), channel_id=1, source_target_pairs={{0,8},{8,16},{16,24},{24,32},{32,40},{40,48},{48,56},{56,64},{64,7... | collective-permute-start | bytes 786440 | tf_op jit(solution)/shard_map/while/body/eval_jaxpr/ppermute | solution.py:15
  181.2 7.9 %collective-permute-start = (bf16[16,8192]{1,0:T(8,128)(2,1)}, bf16[16,8192]{1,0:T(8,128)(2,1)S(1)}, u32[]{:S(2)}, u32[]{:S(2)}) collective-permute-start(bf16[16,8192]{1,0:T(8,128)(2,1)} %get-tuple-element.278), channel_id=1, source_target_pairs={{0,8},{8,16},{16,24},{24,32},{32,40},{40,48},{48,56},{56,64},{64,7... | collective-permute-start | bytes 786440 | tf_op jit(solution)/shard_map/while/body/eval_jaxpr/ppermute | solution.py:15
  194.0 8.6 %collective-permute-start = (bf16[16,8192]{1,0:T(8,128)(2,1)}, bf16[16,8192]{1,0:T(8,128)(2,1)S(1)}, u32[]{:S(2)}, u32[]{:S(2)}) collective-permute-start(bf16[16,8192]{1,0:T(8,128)(2,1)} %get-tuple-element.278), channel_id=1, source_target_pairs={{0,8},{8,16},{16,24},{24,32},{32,40},{40,48},{48,56},{56,64},{64,7... | collective-permute-start | bytes 786440 | tf_op jit(solution)/shard_map/while/body/eval_jaxpr/ppermute | solution.py:15
  207.6 10.0 %collective-permute-start = (bf16[16,8192]{1,0:T(8,128)(2,1)}, bf16[16,8192]{1,0:T(8,128)(2,1)S(1)}, u32[]{:S(2)}, u32[]{:S(2)}) collective-permute-start(bf16[16,8192]{1,0:T(8,128)(2,1)} %get-tuple-element.278), channel_id=1, source_target_pairs={{0,8},{8,16},{16,24},{24,32},{32,40},{40,48},{48,56},{56,64},{64,7... | collective-permute-start | bytes 786440 | tf_op jit(solution)/shard_map/while/body/eval_jaxpr/ppermute | solution.py:15
  222.5 10.0 %collective-permute-start = (bf16[16,8192]{1,0:T(8,128)(2,1)}, bf16[16,8192]{1,0:T(8,128)(2,1)S(1)}, u32[]{:S(2)}, u32[]{:S(2)}) collective-permute-start(bf16[16,8192]{1,0:T(8,128)(2,1)} %get-tuple-element.278), channel_id=1, source_target_pairs={{0,8},{8,16},{16,24},{24,32},{32,40},{40,48},{48,56},{56,64},{64,7... | collective-permute-start | bytes 786440 | tf_op jit(solution)/shard_map/while/body/eval_jaxpr/ppermute | solution.py:15
  237.5 10.0 %collective-permute-start = (bf16[16,8192]{1,0:T(8,128)(2,1)}, bf16[16,8192]{1,0:T(8,128)(2,1)S(1)}, u32[]{:S(2)}, u32[]{:S(2)}) collective-permute-start(bf16[16,8192]{1,0:T(8,128)(2,1)} %get-tuple-element.278), channel_id=1, source_target_pairs={{0,8},{8,16},{16,24},{24,32},{32,40},{40,48},{48,56},{56,64},{64,7... | collective-permute-start | bytes 786440 | tf_op jit(solution)/shard_map/while/body/eval_jaxpr/ppermute | solution.py:15
  252.5 10.0 %collective-permute-start = (bf16[16,8192]{1,0:T(8,128)(2,1)}, bf16[16,8192]{1,0:T(8,128)(2,1)S(1)}, u32[]{:S(2)}, u32[]{:S(2)}) collective-permute-start(bf16[16,8192]{1,0:T(8,128)(2,1)} %get-tuple-element.278), channel_id=1, source_target_pairs={{0,8},{8,16},{16,24},{24,32},{32,40},{40,48},{48,56},{56,64},{64,7... | collective-permute-start | bytes 786440 | tf_op jit(solution)/shard_map/while/body/eval_jaxpr/ppermute | solution.py:15
  267.4 10.0 %collective-permute-start = (bf16[16,8192]{1,0:T(8,128)(2,1)}, bf16[16,8192]{1,0:T(8,128)(2,1)S(1)}, u32[]{:S(2)}, u32[]{:S(2)}) collective-permute-start(bf16[16,8192]{1,0:T(8,128)(2,1)} %get-tuple-element.278), channel_id=1, source_target_pairs={{0,8},{8,16},{16,24},{24,32},{32,40},{40,48},{48,56},{56,64},{64,7... | collective-permute-start | bytes 786440 | tf_op jit(solution)/shard_map/while/body/eval_jaxpr/ppermute | solution.py:15
  282.4 10.0 %collective-permute-start = (bf16[16,8192]{1,0:T(8,128)(2,1)}, bf16[16,8192]{1,0:T(8,128)(2,1)S(1)}, u32[]{:S(2)}, u32[]{:S(2)}) collective-permute-start(bf16[16,8192]{1,0:T(8,128)(2,1)} %get-tuple-element.278), channel_id=1, source_target_pairs={{0,8},{8,16},{16,24},{24,32},{32,40},{40,48},{48,56},{56,64},{64,7... | collective-permute-start | bytes 786440 | tf_op jit(solution)/shard_map/while/body/eval_jaxpr/ppermute | solution.py:15
  297.4 10.0 %collective-permute-start = (bf16[16,8192]{1,0:T(8,128)(2,1)}, bf16[16,8192]{1,0:T(8,128)(2,1)S(1)}, u32[]{:S(2)}, u32[]{:S(2)}) collective-permute-start(bf16[16,8192]{1,0:T(8,128)(2,1)} %get-tuple-element.278), channel_id=1, source_target_pairs={{0,8},{8,16},{16,24},{24,32},{32,40},{40,48},{48,56},{56,64},{64,7... | collective-permute-start | bytes 786440 | tf_op jit(solution)/shard_map/while/body/eval_jaxpr/ppermute | solution.py:15
  312.3 10.0 %collective-permute-start = (bf16[16,8192]{1,0:T(8,128)(2,1)}, bf16[16,8192]{1,0:T(8,128)(2,1)S(1)}, u32[]{:S(2)}, u32[]{:S(2)}) collective-permute-start(bf16[16,8192]{1,0:T(8,128)(2,1)} %get-tuple-element.278), channel_id=1, source_target_pairs={{0,8},{8,16},{16,24},{24,32},{32,40},{40,48},{48,56},{56,64},{64,7... | collective-permute-start | bytes 786440 | tf_op jit(solution)/shard_map/while/body/eval_jaxpr/ppermute | solution.py:15
  326.7 378.8 %reduce-scatter.2.cloned.1.call-start = ((), (), s32[]{:S(2)}) async-start(), calls=%async_computation.2 | async-start | bytes 2359296 | tf_op jit(solution)/shard_map/reduce_scatter | solution.py:89
  632.6 0.7 copy-start.8
  632.6 6.3 copy-start.7
  632.6 73.0 %copy-start.6 = (f32[512]{0:T(512)S(1)}, f32[512]{0:T(512)}, u32[]{:S(2)}) copy-start(f32[512]{0:T(512)} %param.13) | copy-start | bytes 6148
  632.6 129.0 %all-gather.2.cloned.1.call-start = ((), (), s32[]{:S(2)}) async-start(), calls=%async_computation.3 | async-start | bytes 1179648 | tf_op jit(solution)/shard_map/all_gather | solution.py:110
  705.6 3.7 copy-start.2
  710.1 2.5 copy-start.3
  761.6 9.4 %copy-start.1 = (bf16[3,1024,512]{2,1,0:T(8,128)(2,1)S(1)}, bf16[3,1024,512]{2,1,0:T(8,128)(2,1)}, u32[]{:S(2)}) copy-start(bf16[3,1024,512]{2,1,0:T(8,128)(2,1)} %param.12) | copy-start | bytes 9437188
Sparse Core Ops, SparseCore 0:
  326.9 166.7 all-reduce.23
  632.7 72.7 reduce-scatter.1
  715.1 46.4 all-gather.1
where the time goes:
time: 781 us; the launch traced here: 778 us
  waiting for transfers between devices  327 us (42%)
  blocking collectives  129 us (17%)
  starting transfers between devices  116 us (15%)
  other arithmetic  98.4 us (13%)
  local copies, waits for them, and re-layouts  67 us (9%)
  between operations  23 us (3%)
  matrix products  16.9 us (2%)
    psum x1, waiting for transfers between devices, from_root(): return lax.psum(jnp.where(mine, value, jnp.zeros_like(value)), axis)  167 us
    ppermute x23, starting transfers between devices, shifted(): lax.ppermute(value, axis, [(source, source + steps) for source in range(f...  116 us
    all_to_all x1, blocking collectives, local(): lax.all_to_all(taps, 'dp', split_axis=2, concat_axis=1, tiled=True)  99.6 us
    ppermute x23, waiting for transfers between devices, shifted(): lax.ppermute(value, axis, [(source, source + steps) for source in range(f...  83 us
    reduce_scatter x1, waiting for transfers between devices, local(): lax.psum_scatter(jnp.einsum('bcr,brd->cd', block, fc_weight, preferred_el...  64.8 us
    dynamic_update_slice x23, other arithmetic, tick_three(): lax.dynamic_update_index_in_dim(outputs, jnp.where(active, result, previo...  49.2 us
    dynamic_slice x23, local copies, waits for them, and re-layouts, tick_three(): previous = lax.dynamic_index_in_dim(outputs, slot, 0, keepdims=False)  38.3 us
    psum x1, blocking collectives, local(): step_loss = lax.psum(partial_losses, 'segment')  29.6 us
  transfers between devices with their start and end apart: 26, of which 26 were waited for; matrix products, arithmetic and copies ran while one was open for 0% of the time, Pallas kernels for 0%

commit v1 on v0

v1 whole, which is shorter than its diff:
```python
import jax
import jax.numpy as jnp
from jax import lax
from jax.sharding import PartitionSpec as P

D = 8192
MB = 16
NMB = 8
STEPS = 7
SECTIONS = 16


def section_step(hidden, gain, mix):
    values = hidden.astype(jnp.float32)
    scale = jnp.sqrt(jnp.mean(values * values, axis=-1, keepdims=True) + 1e-05)
    return (values + mix * jax.nn.silu(gain * values / scale)).astype(jnp.bfloat16)


def unroll_losses(joined, upper, decay, tok_len, masks, width):
    count_tok = joined.shape[0]
    columns = joined.shape[1]
    position = jnp.arange(count_tok, dtype=jnp.int32) % MB
    keep_prev = (position >= 1).astype(jnp.float32)[:, None]
    state = joined
    losses = []
    for step in range(1, STEPS + 1):
        before = jnp.concatenate([jnp.zeros((1, columns), jnp.float32), state[:-1]], 0) * keep_prev
        state = joined + decay[None, :] * masks[step - 1].astype(jnp.float32)[:, None] * before
        target = jnp.concatenate([upper[step:], jnp.zeros((step, columns), jnp.float32)], 0)
        weight = (position + step < tok_len).astype(jnp.float32)
        count = jnp.sum(weight)
        differ = state - target
        total = jnp.sum(weight[:, None] * differ * differ)
        losses.append(total / (width * jnp.maximum(count, 1.0)))
    return jnp.stack(losses)


def local(stream_in, sec_gain, sec_mix, fc_weight, decay, lengths, ttt_mask):
    seg = lax.axis_index("segment")
    n_seg = lax.axis_size("segment")
    tok = stream_in.shape[0]
    own = tok // n_seg
    params = lax.all_gather(jnp.concatenate([sec_gain, sec_mix]), "segment", axis=0, tiled=False)
    hidden = lax.dynamic_slice_in_dim(stream_in, seg * own, own, 0)
    taps = []
    for s in range(SECTIONS):
        hidden = section_step(hidden, params[s, 0], params[s, 1])
        if s in (0, SECTIONS // 2, SECTIONS - 1):
            taps.append(hidden)
    taps = jnp.stack(taps)
    mine = lax.all_to_all(taps, "dp", split_axis=2, concat_axis=1, tiled=True)
    n_dp = lax.axis_size("dp")
    out_cols = fc_weight.shape[2]
    features = lax.all_gather(mine, "segment", axis=0, tiled=False)
    features = features.reshape(n_seg, 3, n_dp, own, fc_weight.shape[1])
    features = features.transpose(1, 2, 0, 3, 4).reshape(3, n_dp * tok, fc_weight.shape[1])
    upper = lax.all_to_all(
        taps[2].reshape(own, n_seg, out_cols), "segment", split_axis=1, concat_axis=0, tiled=True
    ).reshape(tok, out_cols).astype(jnp.float32)
    joined = lax.psum_scatter(
        jnp.einsum("bcr,brd->cd", features, fc_weight, preferred_element_type=jnp.float32),
        "dp",
        scatter_dimension=0,
        tiled=True,
    )
    tok_len = jnp.repeat(lengths[0], MB)

    def local_objective(joined_local):
        partial_losses = unroll_losses(joined_local, upper, decay, tok_len, ttt_mask, D)
        return (jnp.sum(partial_losses), partial_losses)

    total, vjp_fn, partial_losses = jax.vjp(local_objective, joined, has_aux=True)
    joined_grad = vjp_fn(jnp.ones_like(total))[0]
    step_loss = lax.psum(partial_losses, "segment")
    grad_rows = joined_grad.astype(jnp.bfloat16)
    rows = lax.all_gather(grad_rows, "dp", axis=0, tiled=True)
    fc_grad = jnp.einsum("bcr,cd->brd", features, rows, preferred_element_type=jnp.float32)
    return (step_loss[None, :], fc_grad)


def solution(mesh):
    in_specs = (
        P("dp", None),
        P("segment", None),
        P("segment", None),
        P(None, "dp", "segment"),
        P("segment"),
        P("dp", None),
        P(None, "dp"),
    )
    out_specs = (P("dp", None), P(None, "dp", "segment"))
    return jax.shard_map(local, mesh=mesh, in_specs=in_specs, out_specs=out_specs, check_vma=False)
```

time: 781 us -> 315 us (0.40)
  waiting for transfers between devices: 327 us -> 147 us
  starting transfers between devices: 116 us -> 5.43 us
  blocking collectives: 129 us -> 44.8 us
  other arithmetic: 98.4 us -> 25.2 us
  local copies, waits for them, and re-layouts: 67 us -> 53.8 us
    psum x1 -> x0, waiting for transfers between devices: 167 us -> none  [from_root(): return lax.psum(jnp.where(mine, value, jnp.zeros_like(value)), axis)]
    ppermute x23 -> x0, starting transfers between devices: 116 us -> none  [shifted(): lax.ppermute(value, axis, [(source, source + steps) for source in range(f...]
    all_to_all x1, blocking collectives: 99.6 us -> 15.4 us  [local(): mine = lax.all_to_all(taps, 'dp', split_axis=2, concat_axis=1, tiled=True)]
    ppermute x23 -> x0, waiting for transfers between devices: 83 us -> none  [shifted(): lax.ppermute(value, axis, [(source, source + steps) for source in range(f...]
    all_gather x1 -> x3, waiting for transfers between devices: 11.8 us -> 87.9 us  [the longest x1 40.4 us: local(): features = lax.all_gather(mine, 'segment', axis=0, tiled=False)]
    dynamic_update_slice x23 -> x0, other arithmetic: 49.2 us -> none  [tick_three(): lax.dynamic_update_index_in_dim(outputs, jnp.where(active, result, previo...]
    dynamic_slice x23 -> x0, local copies, waits for them, and re-layouts: 38.3 us -> none  [tick_three(): previous = lax.dynamic_index_in_dim(outputs, slot, 0, keepdims=False)]
    unnamed x18 -> x38, local copies, waits for them, and re-layouts: 0.61 us -> 22.4 us
  transfers between devices with their start and end apart: 26 -> 5, of which waited for: 26 -> 5; matrix products, arithmetic and copies ran while one was open for 0% -> 3% of each run, Pallas kernels for 0% -> 0%
where the time goes in v1:
time: 315 us; the launch traced here: 314 us
  waiting for transfers between devices  147 us (47%)
  local copies, waits for them, and re-layouts  53.8 us (17%)
  blocking collectives  44.8 us (14%)
  other arithmetic  25.2 us (8%)
  between operations  23.1 us (7%)
  matrix products  13.9 us (4%)
  starting transfers between devices  5.43 us (2%)
    reduce_scatter x1, waiting for transfers between devices, local(): lax.psum_scatter(jnp.einsum('bcr,brd->cd', features, fc_weight, preferred...  53.6 us
    all_gather x1, waiting for transfers between devices, local(): features = lax.all_gather(mine, 'segment', axis=0, tiled=False)  40.4 us
    all_gather x1, waiting for transfers between devices, local(): lax.all_gather(jnp.concatenate([sec_gain, sec_mix]), 'segment', axis=0, t...  36.4 us
    psum x1, blocking collectives, local(): step_loss = lax.psum(partial_losses, 'segment')  29.4 us
    unnamed x38, local copies, waits for them, and re-layouts  22.4 us
    all_to_all x1, blocking collectives, local(): mine = lax.all_to_all(taps, 'dp', split_axis=2, concat_axis=1, tiled=True)  15.4 us
    reduce_sum x7, other arithmetic, unroll_losses(): total = jnp.sum(weight[:, None] * differ * differ)  12 us
    all_to_all x1, local copies, waits for them, and re-layouts, local(): mine = lax.all_to_all(taps, 'dp', split_axis=2, concat_axis=1, tiled=True)  11.5 us
  transfers between devices with their start and end apart: 5, of which 5 were waited for; matrix products, arithmetic and copies ran while one was open for 3% of the time, Pallas kernels for 0%

profile of v1, /device:TPU:1, one launch (start us, length us, event | category | flops | bytes accessed | tf_op | source)
XLA Modules:
  0.0 313.6 jit_solution(12364468014140659657)
XLA Ops:
  7.2 1.6 maximum_bitcast_fusion
  8.9 1.1 fusion.23
  10.0 36.4 %all-gather.10.cloned.1.call-done = f32[16,2,8192]{2,1,0:T(2,128)} async-done(((f32[1,2,8192]{2,1,0:T(2,128)}), f32[16,2,8192]{2,1,0:T(2,128)}) %all-gather.10.cloned.1.call-update) | async-done | bytes 1048592 | tf_op jit(solution)/shard_map/all_gather | solution.py:43
  46.4 1.6 fusion.94
  48.0 1.2 fusion.26
  49.3 0.3 fusion.29
  49.6 0.3 fusion.32
  49.9 0.3 fusion.35
  50.2 0.3 fusion.38
  50.5 0.3 fusion.41
  50.8 2.0 fusion.93
  53.4 0.3 fusion.50
  53.8 0.3 fusion.53
  55.0 0.3 fusion.65
  55.4 0.3 fusion.68
  55.9 0.4 copy-done.8
  56.4 8.2 %copy.19 = bf16[3,8,8192]{1,0,2:T(4,128)(2,1)} copy(bf16[3,8,8192]{2,1,0:T(8,128)(2,1)S(1)} %pad_maximum_fusion) | data formatting | bytes 786432 | tf_op jit(solution)/shard_map/stack | solution.py:50
  64.5 9.6 %reshape.315 = bf16[8,2,12288]{2,1,0:T(2,128)(2,1)S(1)} reshape(bf16[8192,3,8]{2,1,0:T(4,128)(2,1)} %bitcast.94) | data formatting | bytes 786432
  74.1 15.4 %all_to_all.24 = bf16[8,2,12288]{2,1,0:T(2,128)(2,1)} all-to-all(bf16[8,2,12288]{2,1,0:T(2,128)(2,1)S(1)} %reshape.315), channel_id=1, replica_groups=mesh['segment'=16,'dp'=8] {'dp'}, dimensions={0} | all-to-all | bytes 786432 | tf_op jit(solution)/shard_map/all_to_all | solution.py:51
  89.5 9.7 %reshape.316 = bf16[8192,3,8]{2,1,0:T(4,128)(2,1)} reshape(bf16[8,2,12288]{2,1,0:T(2,128)(2,1)} %all_to_all.24) | data formatting | bytes 786432
  99.1 11.5 %copy.20 = bf16[3,8,8,1024]{3,2,1,0:T(8,128)(2,1)} copy(bf16[3,8,8,1024]{2,0,3,1:T(4,128)(2,1)} %bitcast.95) | data formatting | bytes 786432 | tf_op jit(solution)/shard_map/all_to_all | solution.py:51
  110.7 40.4 %all-gather.6.cloned.1.call-done = bf16[16,3,64,1024]{3,2,1,0:T(8,128)(2,1)} async-done(((bf16[1,3,64,1024]{3,2,1,0:T(8,128)(2,1)}), bf16[16,3,64,1024]{3,2,1,0:T(8,128)(2,1)}) %all-gather.6.cloned.1.call-update) | async-done | bytes 6291472 | tf_op jit(solution)/shard_map/all_gather | solution.py:54
  151.1 3.5 %copy.21 = bf16[3,8,16,8,1024]{4,3,2,1,0:T(8,128)(2,1)S(1)} copy(bf16[3,8,16,8,1024]{4,3,1,0,2:T(8,128)(2,1)} %bitcast.99) | data formatting | bytes 12582912 | tf_op jit(solution)/shard_map/transpose | solution.py:56
  154.6 2.7 copy-done.2
  157.3 4.7 %convolution_bitcast_fusion = f32[1024,512]{1,0:T(8,128)} fusion(bf16[3,1024,1024]{2,1,0:T(8,128)(2,1)S(1)} %bitcast.97, bf16[3,1024,512]{2,1,0:T(8,128)(2,1)S(1)} %copy-done), kind=kOutput, calls=%fused_computation | convolution fusion | flops 3221225472 | bytes 11534336 | tf_op jit(solution)/shard_map/bcr,brd->cd/dot_general | solution.py:61
  162.2 0.7 convert_reduce_fusion
  167.7 0.8 fusion.69
  168.6 5.1 %all-to-all-start.1 = ((bf16[8,16,512]{2,0,1:T(8,128)(2,1)}), bf16[8,16,512]{2,0,1:T(8,128)(2,1)S(1)}, u32[]{:S(2)}, u32[]{:S(2)}) async-start(bf16[8,16,512]{2,0,1:T(8,128)(2,1)} %bitcast.45), calls=%async_computation.2 | async-start | bytes 262144 | tf_op jit(solution)/shard_map/all_to_all | solution.py:57
  173.9 5.8 %all-to-all-done.1 = bf16[8,16,512]{2,0,1:T(8,128)(2,1)S(1)} async-done(((bf16[8,16,512]{2,0,1:T(8,128)(2,1)}), bf16[8,16,512]{2,0,1:T(8,128)(2,1)S(1)}, u32[]{:S(2)}, u32[]{:S(2)}) %all-to-all-start.1) | async-done | bytes 131104 | tf_op jit(solution)/shard_map/all_to_all | solution.py:57
  179.8 0.7 slice.247
  180.5 0.7 slice.249
  181.3 0.7 slice.251
  182.0 0.7 slice.253
  182.7 0.7 slice.255
  183.5 0.7 slice.257
  184.2 53.6 %reduce-scatter.2.cloned.1.call-done = f32[128,512]{1,0:T(8,128)} async-done(((f32[1024,512]{1,0:T(8,128)}), f32[128,512]{1,0:T(8,128)}) %reduce-scatter.2.cloned.1.call-update) | async-done | bytes 262160 | tf_op jit(solution)/shard_map/reduce_scatter | solution.py:60
  237.8 1.9 fusion.2
  239.7 1.9 fusion.5
  241.6 1.9 fusion.8
  243.5 1.8 fusion.11
  245.3 1.9 fusion.14
  247.3 0.8 fusion.17
  248.1 0.8 fusion.21
  250.4 0.8 add_convert_fusion
  255.0 1.7 fusion.20
  257.4 29.4 %psum.7 = f32[1,7]{1,0:T(1,128)} all-reduce(f32[1,7]{1,0:T(1,128)S(1)} %bitcast.145), channel_id=1, replica_groups=mesh['segment'=16,'dp'=8] {'segment'}, use_global_device_ids=true, to_apply=%region_31.32 | all-reduce | flops 7 | bytes 56 | tf_op jit(solution)/shard_map/psum | solution.py:74
  286.7 11.1 %all-gather.8.cloned.1.call-done = bf16[1024,512]{1,0:T(8,128)(2,1)} async-done(((bf16[128,512]{1,0:T(8,128)(2,1)}), bf16[1024,512]{1,0:T(8,128)(2,1)}) %all-gather.8.cloned.1.call-update) | async-done | bytes 1048592 | tf_op jit(solution)/shard_map/all_gather | solution.py:76
  297.9 9.2 %fusion = f32[3,1024,512]{2,1,0:T(8,128)} fusion(bf16[3,1024,1024]{2,1,0:T(8,128)(2,1)} %bitcast.98, bf16[1024,512]{1,0:T(8,128)(2,1)} %all-gather.8.cloned.1.call-done), kind=kOutput, calls=%fused_computation.1 | convolution fusion | flops 3221225472 | bytes 13631488 | tf_op jit(solution)/shard_map/bcr,cd->brd/dot_general | solution.py:77
  (87 shorter events, 4.1 us)
Async XLA Ops:
  7.2 150.1 %copy-start = (bf16[3,1024,512]{2,1,0:T(8,128)(2,1)S(1)}, bf16[3,1024,512]{2,1,0:T(8,128)(2,1)}, u32[]{:S(2)}) copy-start(bf16[3,1024,512]{2,1,0:T(8,128)(2,1)} %param.10) | copy-start | bytes 9437188
  7.2 39.2 %all-gather.10.cloned.1.call-start = ((), (), s32[]{:S(2)}) async-start(), calls=%async_computation.6 | async-start | bytes 1114112 | tf_op jit(solution)/shard_map/all_gather | solution.py:43
  8.9 142.2 %all-gather.6.cloned.1.call-start = ((), (), s32[]{:S(2)}) async-start(), calls=%async_computation.3 | async-start | bytes 6684672 | tf_op jit(solution)/shard_map/all_gather | solution.py:54
  48.0 8.3 %copy-start.13 = (f32[1,1,8192]{2,1,0:T(1,128)}, f32[1,1,8192]{2,1,0:T(1,128)S(1)}, u32[]{:S(2)}) copy-start(f32[1,1,8192]{2,1,0:T(1,128)S(1)} %get-tuple-element.72) | copy-start | bytes 98308
  52.8 3.5 %copy-start.11 = (f32[1,1,8192]{2,1,0:T(1,128)}, f32[1,1,8192]{2,1,0:T(1,128)S(1)}, u32[]{:S(2)}) copy-start(f32[1,1,8192]{2,1,0:T(1,128)S(1)} %get-tuple-element.53) | copy-start | bytes 98308
  55.7 0.6 copy-start.8
  110.7 127.1 %reduce-scatter.2.cloned.1.call-start = ((), (), s32[]{:S(2)}) async-start(), calls=%async_computation.4 | async-start | bytes 2359296 | tf_op jit(solution)/shard_map/reduce_scatter | solution.py:60
  154.6 2.7 copy-start.2
  157.3 4.8 %copy-start.17 = (s32[1,8]{1,0:T(1,128)S(1)}, s32[1,8]{1,0:T(1,128)}, u32[]{:S(2)}) copy-start(s32[1,8]{1,0:T(1,128)} %param.12) | copy-start | bytes 100
  157.3 10.4 %copy-start.16 = (s32[7,128]{1,0:T(8,128)S(1)}, s32[7,128]{1,0:T(8,128)}, u32[]{:S(2)}) copy-start(s32[7,128]{1,0:T(8,128)} %param.13) | copy-start | bytes 10756
  157.3 10.5 %copy-start.9 = (bf16[8,8192]{1,0:T(8,128)(2,1)S(1)}, bf16[8,8192]{1,0:T(8,128)(2,1)}, u32[]{:S(2)}) copy-start(bf16[8,8192]{1,0:T(8,128)(2,1)} %copy-done.8) | copy-start | bytes 393220
  157.3 10.5 %copy-start.12 = (f32[1,1,8192]{2,1,0:T(1,128)S(1)}, f32[1,1,8192]{2,1,0:T(1,128)}, u32[]{:S(2)}) copy-start(f32[1,1,8192]{2,1,0:T(1,128)} %copy-done.11) | copy-start | bytes 98308
  157.3 10.5 %copy-start.14 = (f32[1,1,8192]{2,1,0:T(1,128)S(1)}, f32[1,1,8192]{2,1,0:T(1,128)}, u32[]{:S(2)}) copy-start(f32[1,1,8192]{2,1,0:T(1,128)} %copy-done.13) | copy-start | bytes 98308
  162.0 75.8 %copy-start.15 = (f32[512]{0:T(512)S(1)}, f32[512]{0:T(512)}, u32[]{:S(2)}) copy-start(f32[512]{0:T(512)} %param.11) | copy-start | bytes 6148
  168.6 11.2 %all-to-all-start.1 = ((bf16[8,16,512]{2,0,1:T(8,128)(2,1)}), bf16[8,16,512]{2,0,1:T(8,128)(2,1)S(1)}, u32[]{:S(2)}, u32[]{:S(2)}) async-start(bf16[8,16,512]{2,0,1:T(8,128)(2,1)} %bitcast.45), calls=%async_computation.2 | async-start | bytes 262144 | tf_op jit(solution)/shard_map/all_to_all | solution.py:57
  173.7 124.2 %all-gather.8.cloned.1.call-start = ((), (), s32[]{:S(2)}) async-start(), calls=%async_computation.5 | async-start | bytes 1179648 | tf_op jit(solution)/shard_map/all_gather | solution.py:76
  237.8 9.5 %copy-start.1 = (f32[128,512]{1,0:T(8,128)S(1)}, f32[128,512]{1,0:T(8,128)}, u32[]{:S(2)}) copy-start(f32[128,512]{1,0:T(8,128)} %reduce-scatter.2.cloned.1.call-done) | copy-start | bytes 786436
  237.8 9.5 %copy-start.7 = (f32[122,512]{1,0:T(8,128)S(1)}, f32[122,512]{1,0:T(8,128)}, u32[]{:S(2)}) copy-start(f32[122,512]{1,0:T(8,128)} %slice.255) | copy-start | bytes 749572
  237.8 10.3 %copy-start.10 = (f32[121,512]{1,0:T(8,128)S(1)}, f32[121,512]{1,0:T(8,128)}, u32[]{:S(2)}) copy-start(f32[121,512]{1,0:T(8,128)} %slice.257) | copy-start | bytes 743428
  237.8 11.5 %copy-start.6 = (f32[123,512]{1,0:T(8,128)S(1)}, f32[123,512]{1,0:T(8,128)}, u32[]{:S(2)}) copy-start(f32[123,512]{1,0:T(8,128)} %slice.253) | copy-start | bytes 755716
  239.7 9.8 %copy-start.5 = (f32[124,512]{1,0:T(8,128)S(1)}, f32[124,512]{1,0:T(8,128)}, u32[]{:S(2)}) copy-start(f32[124,512]{1,0:T(8,128)} %slice.251) | copy-start | bytes 761860
  241.6 8.2 %copy-start.4 = (f32[125,512]{1,0:T(8,128)S(1)}, f32[125,512]{1,0:T(8,128)}, u32[]{:S(2)}) copy-start(f32[125,512]{1,0:T(8,128)} %slice.249) | copy-start | bytes 768004
  245.3 4.6 %copy-start.3 = (f32[126,512]{1,0:T(8,128)S(1)}, f32[126,512]{1,0:T(8,128)}, u32[]{:S(2)}) copy-start(f32[126,512]{1,0:T(8,128)} %slice.247) | copy-start | bytes 774148
Sparse Core Ops, SparseCore 0:
  10.3 36.0 all-gather.9
  110.8 40.2 all-gather.5
  162.1 75.5 reduce-scatter.1
  251.3 46.4 all-gather.7

commit v2 on v1

v2 whole, which is shorter than its diff:
```python
import functools

import jax
import jax.numpy as jnp
from jax import lax
from jax.experimental import pallas as pl
from jax.experimental.pallas import tpu as pltpu
from jax.sharding import PartitionSpec as P

D = 8192
MB = 16
NMB = 8
STEPS = 7
SECTIONS = 16
TAPS = (0, SECTIONS // 2, SECTIONS - 1)
TOK = 128
SEG = 16
DP = 8
IN = D // DP
OUT = D // SEG
OWN = TOK // SEG
F32 = jnp.float32
BF16 = jnp.bfloat16
MESH = pl.DeviceIdType.MESH


def at(segment, dp):
    return {"segment": segment, "dp": dp}


def advance(h, half_gain, mix, inv):
    u = (h * half_gain) * inv
    return (h + (mix * u) * (1.0 + jnp.tanh(u))).astype(BF16)


def run_sections(h, inv_cols, gain_of, mix_of):
    rows = h.shape[0]
    taps = []
    for sec in range(SECTIONS):
        gain = jnp.concatenate([gain_of(sec)] * (rows // 8), 0)
        mix = jnp.concatenate([mix_of(sec)] * (rows // 8), 0)
        out = advance(h, gain, mix, inv_cols[:, sec:sec + 1])
        if sec in TAPS:
            taps.append(out)
        h = out.astype(F32)
    return taps


def kernel(stream, gain, mix, weight, decay, lengths, mask, loss_out, grad_out,
           gain_all, mix_all, gain_b, mix_b, gain_u, mix_u, rows16, hx, h0, tile, sc1, packed, sc2, inv_own, inv_j,
           w, feat, feat_t, stage, parts, own_part, up_in, upper, mask_t, mask_pad, left, loss_acc, loss_tile,
           loss_all, rows_own, rows_all, grad,
           in_sem, g_send, m_send, g_recv, m_recv, gf_send, mf_send, h_send, h_recv, r1_send, r1_recv, r2_send,
           r2_recv, f_send, f_recv, p_send, p_recv, q_send, q_recv, l_send, l_recv, o_sem):
    s = lax.axis_index("segment")
    d = lax.axis_index("dp")
    c = lax.rem(s, 2)
    sib = s + 1 - 2 * c
    home = lax.rem(d, 2) == c
    seg_peers = [lax.rem(s + i, SEG) for i in range(1, SEG)]
    dp_peers = [lax.rem(d + i, DP) for i in range(1, DP)]
    remote = functools.partial(pltpu.make_async_remote_copy, device_id_type=MESH)

    w_copies = [
        pltpu.make_async_copy(weight.at[i], w.at[pl.ds(i * IN, IN)], in_sem.at[i]) for i in range(3)
    ]
    row0 = pl.multiple_of((s // 2) * 16, 16)
    rows_copy = pltpu.make_async_copy(stream.at[pl.ds(row0, 16)], rows16, in_sem.at[3])
    up_copy = pltpu.make_async_copy(
        stream.at[:, pl.ds(pl.multiple_of(s * OUT, OUT), OUT)], up_in, in_sem.at[4]
    )
    rows_copy.start()
    gain_copy = pltpu.make_async_copy(gain, gain_all.at[s], g_recv.at[s])
    mix_copy = pltpu.make_async_copy(mix, mix_all.at[s], m_recv.at[s])
    gain_copy.start()
    mix_copy.start()

    barrier = pltpu.get_barrier_semaphore()
    for peer in seg_peers:
        pl.semaphore_signal(barrier, inc=1, device_id=at(peer, d), device_id_type=MESH)
    for peer in dp_peers:
        pl.semaphore_signal(barrier, inc=1, device_id=at(s, peer), device_id_type=MESH)
    pl.semaphore_wait(barrier, SEG - 1 + DP - 1)

    first = [sib] + [lax.rem(s + 2 * i, SEG) for i in range(1, SEG // 2)]
    g_sends = []
    for i, peer in enumerate(first):
        for src, dst, snd, rcv in ((gain, gain_all, g_send, g_recv), (mix, mix_all, m_send, m_recv)):
            copy = remote(src, dst.at[s], snd.at[i], rcv.at[s], device_id=at(peer, d))
            copy.start()
            g_sends.append(copy)

    def h_copy(i):
        peer = lax.rem(d + i, DP)
        return remote(
            stream.at[:, pl.ds(pl.multiple_of(peer * IN, IN), IN)], h0.at[d // 2],
            h_send.at[i], h_recv.at[d // 2], device_id=at(s, peer),
        )

    @pl.when(home)
    def _():
        for i in range(1, DP):
            h_copy(i).start()
        pltpu.make_async_copy(
            stream.at[:, pl.ds(pl.multiple_of(d * IN, IN), IN)], h0.at[d // 2], h_recv.at[d // 2]
        ).start()

    up_copy.start()
    for copy in w_copies:
        copy.start()

    token = lax.broadcasted_iota(jnp.int32, (TOK, 128), 0)
    pos = token & (MB - 1)
    micro = lax.shift_right_logical(token, 4)
    tok_len = jnp.zeros((TOK, 128), jnp.int32)
    for m in range(NMB):
        tok_len = jnp.where(micro == m, lengths[0, m], tok_len)
    left[...] = tok_len - pos
    mask_pad[...] = jnp.zeros_like(mask_pad)
    mask_pad[0:STEPS, :] = mask[...].astype(F32)
    mask_t[...] = jnp.where(pos >= 1, mask_pad[...].T, 0.0)
    loss_acc[...] = jnp.zeros_like(loss_acc)

    def wait_param(slot):
        remote(gain, gain_all.at[slot], g_send.at[0], g_recv.at[slot], device_id=at(sib, d)).wait_recv()
        remote(mix, mix_all.at[slot], m_send.at[0], m_recv.at[slot], device_id=at(sib, d)).wait_recv()

    for i in range(1, SEG // 2):
        slot = lax.rem(s + 2 * i, SEG)
        wait_param(slot)
        for dst, snd, rcv in ((gain_all, gf_send, g_recv), (mix_all, mf_send, m_recv)):
            copy = remote(dst.at[slot], dst.at[slot], snd.at[i], rcv.at[slot], device_id=at(sib, d))
            copy.start()
            g_sends.append(copy)
    gain_copy.wait()
    mix_copy.wait()
    wait_param(sib)
    for i in range(1, SEG // 2):
        wait_param(lax.rem(sib + 2 * i, SEG))

    rows_copy.wait()
    hx[...] = rows16[...].astype(F32)
    half = pl.ds(pl.multiple_of(c * OWN, OWN), OWN)
    lane = lax.broadcasted_iota(jnp.int32, (OWN, 128), 1)

    def inverse(h):
        return lax.rsqrt(jnp.sum(h * h, axis=1, keepdims=True) * (1.0 / D) + 1e-05)

    def scale_step(sec, carry):
        inv, acc = carry
        acc = jnp.where(lane == sec, inv, acc)
        h = advance(hx[half, :], 0.5 * gain_all[sec], mix_all[sec], inv).astype(F32)
        hx[half, :] = h
        return inverse(h), acc

    inv, acc = lax.fori_loop(
        0, SECTIONS - 1, scale_step, (inverse(hx[half, :]), jnp.zeros((OWN, 128), F32))
    )
    tile[...] = jnp.where(lane == SECTIONS - 1, inv, acc)
    sc1[s] = tile[...]
    r1_sends = []
    for i, peer in enumerate(seg_peers):
        copy = remote(tile, sc1.at[s], r1_send.at[i], r1_recv.at[s], device_id=at(peer, d))
        copy.start()
        r1_sends.append(copy)

    def spread(sec, _):
        g = 0.5 * gain_all[sec]
        m = mix_all[sec]
        gain_b[sec] = jnp.broadcast_to(0.5 * gain_all[sec, :, pl.ds(pl.multiple_of(d * IN, IN), IN)], (8, IN))
        mix_b[sec] = jnp.broadcast_to(mix_all[sec, :, pl.ds(pl.multiple_of(d * IN, IN), IN)], (8, IN))
        gain_u[sec] = jnp.broadcast_to(0.5 * gain_all[sec, :, pl.ds(pl.multiple_of(s * OUT, OUT), OUT)], (8, OUT))
        mix_u[sec] = jnp.broadcast_to(mix_all[sec, :, pl.ds(pl.multiple_of(s * OUT, OUT), OUT)], (8, OUT))
        return 0

    lax.fori_loop(0, SECTIONS, spread, 0)
    for i, peer in enumerate(seg_peers):
        remote(tile, sc1.at[peer], r1_send.at[i], r1_recv.at[peer], device_id=at(peer, d)).wait_recv()
    inv_own[...] = sc1[...].reshape(TOK, 128)
    packed[...] = inv_own[...].T[0:SECTIONS, :]

    def r2_copy(i):
        peer = lax.rem(d + i, DP)
        return remote(packed, sc2.at[d], r2_send.at[i], r2_recv.at[d], device_id=at(s, peer))

    @pl.when(home)
    def _():
        for i in range(1, DP):
            r2_copy(i).start()
        sc2[d] = packed[...]

    for copy in w_copies:
        copy.wait()

    def replica_of(first_home, n):
        base = jnp.where(first_home, d, d + 1)
        return lax.rem(base + 2 * n, DP)

    def p_copy(j):
        return remote(stage.at[j], parts.at[d], p_send.at[j], p_recv.at[d], device_id=at(s, j))

    def join(j):
        rows = pl.ds(pl.multiple_of(j * TOK, TOK), TOK)
        part = jnp.dot(feat[rows, :], w[...], preferred_element_type=F32)

        @pl.when(j == d)
        def _():
            own_part[...] = part

        @pl.when(j != d)
        def _():
            stage[j] = part.astype(BF16)
            p_copy(j).start()

    def f_copy(j):
        rows = pl.ds(pl.multiple_of(j * TOK, TOK), TOK)
        return remote(feat.at[rows], feat.at[rows], f_send.at[j // 2], f_recv.at[j // 2], device_id=at(sib, d))

    def work(n, _):
        j = replica_of(home, n)
        slot = j // 2
        remote(
            stream.at[:, pl.ds(0, IN)], h0.at[slot], h_send.at[0], h_recv.at[slot], device_id=at(sib, d)
        ).wait_recv()

        @pl.when(j != d)
        def _():
            remote(packed, sc2.at[j], r2_send.at[0], r2_recv.at[j], device_id=at(s, j)).wait_recv()

        inv_j[...] = jnp.concatenate([sc2[j], jnp.zeros((128 - SECTIONS, 128), F32)], 0).T

        def one(t, _):
            r = pl.multiple_of((t // 2) * 32, 32)
            col = pl.multiple_of((t % 2) * 512, 512)
            cols = pl.ds(col, 512)
            taps = run_sections(
                h0[slot, pl.ds(r, 32), cols].astype(F32), inv_j[pl.ds(r, 32), :],
                lambda sec: gain_b[sec, :, cols], lambda sec: mix_b[sec, :, cols],
            )
            for i, tap in enumerate(taps):
                feat[pl.ds(pl.multiple_of(j * TOK + r, 32), 32), pl.ds(pl.multiple_of(i * IN + col, 512), 512)] = tap
            return 0

        lax.fori_loop(0, 8, one, 0)
        f_copy(j).start()
        join(j)
        return 0

    lax.fori_loop(1, 5, work, 0)

    def other(n, _):
        j = replica_of(jnp.logical_not(home), n)
        f_copy(j).wait_recv()
        join(j)
        return 0

    lax.fori_loop(1, 5, other, 0)

    up_copy.wait()

    def up_one(t, _):
        rows = pl.ds(pl.multiple_of(t * 32, 32), 32)
        taps = run_sections(
            up_in[rows, :].astype(F32), inv_own[rows, :], lambda sec: gain_u[sec], lambda sec: mix_u[sec]
        )
        upper[rows, :] = taps[2].astype(F32)
        return 0

    lax.fori_loop(0, 4, up_one, 0)

    def turn(t, _):
        rows = pl.ds(pl.multiple_of((t % 8) * TOK, TOK), TOK)
        cols = pl.ds(pl.multiple_of((t // 8) * 512, 512), 512)
        feat_t[cols, rows] = feat[rows, cols].T
        return 0

    lax.fori_loop(0, 48, turn, 0)

    for peer in dp_peers:
        remote(stage.at[peer], parts.at[peer], p_send.at[peer], p_recv.at[peer], device_id=at(s, peer)).wait_recv()

    inv_count = []
    for k in range(1, STEPS + 1):
        count = jnp.int32(0)
        for m in range(NMB):
            count = count + jnp.maximum(lengths[0, m] - k, 0)
        inv_count.append(1.0 / (jnp.full((1, 128), jnp.maximum(count, 1), jnp.int32).astype(F32) * D))

    def draft(q, _):
        cols = pl.ds(pl.multiple_of(q * 128, 128), 128)
        joined = own_part[:, cols]
        for peer in dp_peers:
            joined = joined + parts[peer, :, cols].astype(F32)
        up = upper[:, cols]
        dec = decay[:, cols]
        plen = left[...]

        def carry_of(k):
            return dec * mask_t[:, k - 1:k]

        state = joined
        pulls = []
        for k in range(1, STEPS + 1):
            state = joined + carry_of(k) * pltpu.roll(state, 1, 0)
            target = pltpu.roll(up, TOK - k, 0)
            diff = jnp.where(plen > k, state - target, 0.0)
            loss_acc[k - 1] += jnp.sum((diff * diff).reshape(TOK // 8, 8, 128), axis=0)
            pulls.append(diff * (2.0 * inv_count[k - 1]))
        back = pulls[STEPS - 1]
        total = back
        for k in range(STEPS - 1, 0, -1):
            back = pulls[k - 1] + pltpu.roll(carry_of(k + 1) * back, TOK - 1, 0)
            total = total + back
        total = total + pltpu.roll(carry_of(1) * back, TOK - 1, 0)
        rows_own[:, cols] = total.astype(BF16)
        return 0

    lax.fori_loop(0, OUT // 128, draft, 0)

    def q_copy(i):
        peer = lax.rem(d + i, DP)
        here = pl.ds(pl.multiple_of(d * TOK, TOK), TOK)
        return remote(rows_own, rows_all.at[here], q_send.at[i], q_recv.at[d], device_id=at(s, peer))

    for i in range(1, DP):
        q_copy(i).start()
    rows_all[pl.ds(pl.multiple_of(d * TOK, TOK), TOK), :] = rows_own[...]

    lane = lax.broadcasted_iota(jnp.int32, (8, 128), 1)
    losses = jnp.zeros((8, 128), F32)
    for k in range(1, STEPS + 1):
        losses = jnp.where(lane == k - 1, jnp.sum(loss_acc[k - 1]) * inv_count[k - 1], losses)
    loss_tile[...] = losses
    loss_all[s] = losses
    l_sends = []
    for i, peer in enumerate(seg_peers):
        copy = remote(loss_tile, loss_all.at[s], l_send.at[i], l_recv.at[s], device_id=at(peer, d))
        copy.start()
        l_sends.append(copy)

    for peer in dp_peers:
        there = pl.ds(pl.multiple_of(peer * TOK, TOK), TOK)
        remote(rows_own, rows_all.at[there], q_send.at[0], q_recv.at[peer], device_id=at(s, peer)).wait_recv()

    def o_copy(t):
        return pltpu.make_async_copy(
            grad.at[t], grad_out.at[t // 4, pl.ds(pl.multiple_of((t % 4) * 256, 256), 256)], o_sem.at[t]
        )

    def finish(t, _):
        rows = pl.ds(pl.multiple_of(t * 256, 256), 256)
        grad[t] = jnp.dot(feat_t[rows, :], rows_all[...], preferred_element_type=F32)
        o_copy(t).start()
        return 0

    lax.fori_loop(0, 12, finish, 0)

    for i, peer in enumerate(seg_peers):
        remote(loss_tile, loss_all.at[peer], l_send.at[i], l_recv.at[peer], device_id=at(peer, d)).wait_recv()
    summed = loss_all[0]
    for i in range(1, SEG):
        summed = summed + loss_all[i]
    loss_out[...] = summed

    for copy in g_sends + r1_sends + l_sends:
        copy.wait_send()

    @pl.when(home)
    def _():
        for i in range(1, DP):
            h_copy(i).wait_send()
            r2_copy(i).wait_send()

    for n in range(1, 5):
        f_copy(replica_of(home, n)).wait_send()
    for peer in dp_peers:
        p_copy(peer).wait_send()
    for i in range(1, DP):
        q_copy(i).wait_send()
    for t in range(12):
        o_copy(t).wait()


def local(stream_in, sec_gain, sec_mix, fc_weight, decay, lengths, ttt_mask):
    vmem = pltpu.VMEM
    dma = pltpu.SemaphoreType.DMA
    scratch = [
        vmem((SECTIONS, 1, D), F32), vmem((SECTIONS, 1, D), F32),
        vmem((SECTIONS, 8, IN), F32), vmem((SECTIONS, 8, IN), F32),
        vmem((SECTIONS, 8, OUT), F32), vmem((SECTIONS, 8, OUT), F32),
        vmem((16, D), BF16), vmem((16, D), F32),
        vmem((4, TOK, IN), BF16),
        vmem((OWN, 128), F32), vmem((SEG, OWN, 128), F32),
        vmem((SECTIONS, 128), F32), vmem((DP, SECTIONS, 128), F32),
        vmem((TOK, 128), F32), vmem((TOK, 128), F32),
        vmem((3 * IN, OUT), BF16),
        vmem((DP * TOK, 3 * IN), BF16), vmem((3 * IN, DP * TOK), BF16),
        vmem((DP, TOK, OUT), BF16), vmem((DP, TOK, OUT), BF16), vmem((TOK, OUT), F32),
        vmem((TOK, OUT), BF16), vmem((TOK, OUT), F32),
        vmem((TOK, 128), F32), vmem((TOK, 128), F32), vmem((TOK, 128), jnp.int32),
        vmem((STEPS, 8, 128), F32), vmem((8, 128), F32), vmem((SEG, 8, 128), F32),
        vmem((TOK, OUT), BF16), vmem((DP * TOK, OUT), BF16),
        vmem((12, 256, OUT), F32),
        dma((5,)), dma((8,)), dma((8,)), dma((SEG,)), dma((SEG,)), dma((8,)), dma((8,)),
        dma((DP,)), dma((4,)), dma((SEG,)), dma((SEG,)), dma((DP,)), dma((DP,)), dma((4,)), dma((4,)),
        dma((DP,)), dma((DP,)), dma((DP,)), dma((DP,)), dma((SEG,)), dma((SEG,)), dma((12,)),
    ]
    any_space = pl.BlockSpec(memory_space=pl.ANY)
    in_vmem = pl.BlockSpec(memory_space=pltpu.VMEM)
    loss, grad = pl.pallas_call(
        kernel,
        out_shape=(
            jax.ShapeDtypeStruct((8, 128), F32),
            jax.ShapeDtypeStruct((3, IN, OUT), F32),
        ),
        in_specs=[any_space, any_space, any_space, any_space, in_vmem,
                  pl.BlockSpec(memory_space=pltpu.SMEM), in_vmem],
        out_specs=(in_vmem, any_space),
        scratch_shapes=scratch,
        compiler_params=pltpu.CompilerParams(
            collective_id=0, has_side_effects=True, vmem_limit_bytes=56 * 1024 * 1024
        ),
        name="window",
    )(stream_in, sec_gain, sec_mix, fc_weight, decay.reshape(1, OUT), lengths, ttt_mask)
    return loss[0:1, 0:STEPS], grad


def solution(mesh):
    in_specs = (
        P("dp", None),
        P("segment", None),
        P("segment", None),
        P(None, "dp", "segment"),
        P("segment"),
        P("dp", None),
        P(None, "dp"),
    )
    out_specs = (P("dp", None), P(None, "dp", "segment"))
    return jax.shard_map(local, mesh=mesh, in_specs=in_specs, out_specs=out_specs, check_vma=False)
```

time: 315 us -> 94.5 us (0.30)
  waiting for transfers between devices: 147 us -> 0 us
  Pallas kernels: 0 us -> 84.9 us
  local copies, waits for them, and re-layouts: 53.8 us -> 7.38 us
  blocking collectives: 44.8 us -> 0 us
  other arithmetic: 25.2 us -> 0 us
  between operations: 23.1 us -> 0.64 us
  matrix products: 13.9 us -> 0 us
  starting transfers between devices: 5.43 us -> 0 us
    all_gather x3 -> x0, waiting for transfers between devices: 87.9 us -> none  [the longest x1 40.4 us: local(): features = lax.all_gather(mine, 'segment', axis=0, tiled=False)]
    pallas_call x0 -> x1, Pallas kernels: none -> 84.9 us  [local(): pl.pallas_call(kernel, out_shape=(jax.ShapeDtypeStruct((8, 128), F32), ja...]
    reduce_scatter x1 -> x0, waiting for transfers between devices: 53.6 us -> none  [local(): lax.psum_scatter(jnp.einsum('bcr,brd->cd', features, fc_weight, preferred...]
    psum x1 -> x0, blocking collectives: 29.4 us -> none  [local(): step_loss = lax.psum(partial_losses, 'segment')]
    reduce_sum x24 -> x0, other arithmetic: 19.3 us -> none  [the longest x7 12 us: unroll_losses(): total = jnp.sum(weight[:, None] * differ * differ)]
    unnamed x38 -> x1, local copies, waits for them, and re-layouts: 22.4 us -> 6.2 us
    all_to_all x1 -> x0, blocking collectives: 15.4 us -> none  [local(): mine = lax.all_to_all(taps, 'dp', split_axis=2, concat_axis=1, tiled=True)]
    dot_general x2 -> x0, matrix products: 13.9 us -> none  [the longest x1 9.21 us: local(): jnp.einsum('bcr,cd->brd', features, rows, preferred_element_type=jnp.floa...]
  transfers between devices with their start and end apart: 5 -> 0, of which waited for: 5 -> 0; matrix products, arithmetic and copies ran while one was open for 3% -> 0% of each run, Pallas kernels for 0% -> 0%
where the time goes in v2:
time: 94.5 us; the launch traced here: 93 us
  Pallas kernels  84.9 us (90%)
  local copies, waits for them, and re-layouts  7.38 us (8%)
    pallas_call x1, Pallas kernels, local(): pl.pallas_call(kernel, out_shape=(jax.ShapeDtypeStruct((8, 128), F32), ja...  84.9 us
    unnamed x1, local copies, waits for them, and re-layouts  6.2 us

profile of v2, /device:TPU:1, one launch (start us, length us, event | category | flops | bytes accessed | tf_op | source)
XLA Modules:
  0.0 93.0 jit_solution(7241769817939426775)
XLA Ops:
  0.6 84.9 %window.1 = (f32[8,128]{1,0:T(8,128)}, f32[3,1024,512]{2,1,0:T(8,128)}) custom-call(bf16[128,8192]{1,0:T(8,128)(2,1)} %stream.1, f32[1,8192]{1,0:T(1,128)} %gain.1, f32[1,8192]{1,0:T(1,128)} %mix.1, bf16[3,1024,512]{2,1,0:T(8,128)(2,1)} %weight.1, f32[1,512]{1,0:T(1,128)} %bitcast.1, s32[1,8]{1,0:T(1,128)} %lengths.1, s32[7,128]{1,0:T(8,128)} %mask.1), custom_call_target="tpu_custom_call" | custom-call | tf_op jit(solution)/shard_map/window/pallas_call | solution.py:410
  85.6 1.2 %slice.3 = f32[1,7]{1,0:T(1,128)} slice(f32[8,128]{1,0:T(8,128)} %get-tuple-element.4), slice={[0:1], [0:7]} | slice | bytes 56 | tf_op jit(solution)/shard_map/slice | solution.py:425
  86.8 6.2 %copy.10 = f32[3,1024,512]{2,1,0:T(8,128)} copy(f32[3,1024,512]{2,1,0:T(8,128)} %get-tuple-element.9) | data formatting | bytes 12582912

commit v3 on v2

v3 whole, which is shorter than its diff:
```python
import functools

import jax
import jax.numpy as jnp
from jax import lax
from jax.experimental import pallas as pl
from jax.experimental.pallas import tpu as pltpu
from jax.sharding import PartitionSpec as P

D = 8192
MB = 16
NMB = 8
STEPS = 7
SECTIONS = 16
TAPS = (0, SECTIONS // 2, SECTIONS - 1)
TOK = 128
SEG = 16
DP = 8
VM1 = 40
VM2 = 32
IN = D // DP
OUT = D // SEG
OWN = TOK // SEG
HALF = OUT // 2
F32 = jnp.float32
BF16 = jnp.bfloat16
MESH = pl.DeviceIdType.MESH


def at(segment, dp):
    return {"segment": segment, "dp": dp}


def advance(h, half_gain, mix, inv):
    u = (h * half_gain) * inv
    return (h + (mix * u) * (1.0 + jnp.tanh(u))).astype(BF16)


def run_sections(h, inv_cols, gain_of, mix_of):
    rows = h.shape[0]
    taps = []
    for sec in range(SECTIONS):
        gain = jnp.concatenate([gain_of(sec)] * (rows // 8), 0)
        mix = jnp.concatenate([mix_of(sec)] * (rows // 8), 0)
        out = advance(h, gain, mix, inv_cols[:, sec:sec + 1])
        if sec in TAPS:
            taps.append(out)
        h = out.astype(F32)
    return taps


def kernel(stream, gain, mix, weight, decay_in, lengths_in, mask_in, loss_out, feat_t, rows_out,
           decay, lengths, mask, params, gain_b, mix_b, gain_u, mix_u, rows16, hx, h0, tile, sc1, packed, sc2, inv_own, inv_j,
           w, feat, stage, keep_a, keep_b, in_a1, in_b1, out_a2, in_a2, out_b2, in_b2, own,
           up_in, upper, mask_t, mask_pad, left, loss_acc, loss_tile, loss_all, rows_all,
           in_sem, g_send, g_recv, gf_send, h_send, h_recv, r1_send, r1_recv, r2_send, r2_recv, f_send, f_recv,
           a1_send, a1_recv, b1_send, b1_recv, a2_send, a2_recv, b2_send, b2_recv,
           q_send, q_recv, qa_send, qa_recv, qb_send, qb_recv, l_send, l_recv):
    s = lax.axis_index("segment")
    d = lax.axis_index("dp")
    c = lax.rem(s, 2)
    y = d // 2
    zh = lax.rem(d, 2)
    pair = d + 1 - 2 * zh
    sib = s + 1 - 2 * c
    home = zh == c
    seg_peers = [lax.rem(s + i, SEG) for i in range(1, SEG)]
    dp_peers = [lax.rem(d + i, DP) for i in range(1, DP)]
    y_peers = [lax.rem(y + i, 4) for i in range(1, 4)]
    plane = (s // 8) * 8
    x_peers = [plane + lax.rem(s - plane + 2 * i, 8) for i in range(1, 4)]
    across = lax.rem(s + 8, SEG)
    remote = functools.partial(pltpu.make_async_remote_copy, device_id_type=MESH)

    gain_copy = pltpu.make_async_copy(gain, params.at[s, 0], in_sem.at[5])
    mix_copy = pltpu.make_async_copy(mix, params.at[s, 1], in_sem.at[6])
    gain_copy.start()
    mix_copy.start()
    w_copies = [
        pltpu.make_async_copy(weight.at[i], w.at[pl.ds(i * IN, IN)], in_sem.at[i]) for i in range(3)
    ]
    row0 = pl.multiple_of((s // 2) * 16, 16)
    rows_copy = pltpu.make_async_copy(stream.at[pl.ds(row0, 16)], rows16, in_sem.at[3])
    up_copy = pltpu.make_async_copy(
        stream.at[:, pl.ds(pl.multiple_of(s * OUT, OUT), OUT)], up_in, in_sem.at[4]
    )
    small = [
        pltpu.make_async_copy(src, dst, in_sem.at[7 + i])
        for i, (src, dst) in enumerate(((decay_in, decay), (lengths_in, lengths), (mask_in, mask)))
    ]
    rows_copy.start()
    for copy in small:
        copy.start()

    barrier = pltpu.get_barrier_semaphore()
    for peer in seg_peers:
        pl.semaphore_signal(barrier, inc=1, device_id=at(peer, d), device_id_type=MESH)
    for peer in dp_peers:
        pl.semaphore_signal(barrier, inc=1, device_id=at(s, peer), device_id_type=MESH)
    gain_copy.wait()
    mix_copy.wait()
    pl.semaphore_wait(barrier, SEG - 1 + DP - 1)

    def g_copy(slot, peer, send):
        return remote(params.at[slot], params.at[slot], send, g_recv.at[slot], device_id=at(peer, d))

    sends = []

    def post(copy):
        copy.start()
        sends.append(copy)

    for i, peer in enumerate([across] + x_peers + [sib]):
        post(g_copy(s, peer, g_send.at[i]))

    def h_copy(i):
        peer = lax.rem(d + i, DP)
        return remote(
            stream.at[:, pl.ds(pl.multiple_of(peer * IN, IN), IN)], h0.at[d // 2],
            h_send.at[i], h_recv.at[d // 2], device_id=at(s, peer),
        )

    @pl.when(home)
    def _():
        for i in range(1, DP):
            h_copy(i).start()
        pltpu.make_async_copy(
            stream.at[:, pl.ds(pl.multiple_of(d * IN, IN), IN)], h0.at[d // 2], h_recv.at[d // 2]
        ).start()

    up_copy.start()
    for copy in w_copies:
        copy.start()

    def wait_param(slot):
        g_copy(slot, sib, g_send.at[0]).wait_recv()

    wait_param(across)
    for i, peer in enumerate(x_peers + [sib]):
        post(g_copy(across, peer, gf_send.at[i]))

    for copy in small:
        copy.wait()
    token = lax.broadcasted_iota(jnp.int32, (TOK, 128), 0)
    pos = token & (MB - 1)
    micro = lax.shift_right_logical(token, 4)
    tok_len = jnp.zeros((TOK, 128), jnp.int32)
    for m in range(NMB):
        tok_len = jnp.where(micro == m, lengths[0, m], tok_len)
    left[...] = tok_len - pos
    mask_pad[...] = jnp.zeros_like(mask_pad)
    mask_pad[0:STEPS, :] = mask[...].astype(F32)
    mask_t[...] = jnp.where(pos >= 1, mask_pad[...].T, 0.0)
    loss_acc[...] = jnp.zeros_like(loss_acc)
    rows_copy.wait()
    hx[...] = rows16[...].astype(F32)

    for i, slot in enumerate(x_peers):
        wait_param(slot)
        post(g_copy(slot, sib, gf_send.at[4 + i]))
    for i, peer in enumerate(x_peers):
        slot = lax.rem(peer + 8, SEG)
        wait_param(slot)
        post(g_copy(slot, sib, gf_send.at[7 + i]))
    for i in range(SEG // 2):
        wait_param(lax.rem(sib + 2 * i, SEG))

    half = pl.ds(pl.multiple_of(c * OWN, OWN), OWN)
    lane = lax.broadcasted_iota(jnp.int32, (OWN, 128), 1)

    def inverse(h):
        return lax.rsqrt(jnp.sum(h * h, axis=1, keepdims=True) * (1.0 / D) + 1e-05)

    def scale_step(sec, carry):
        inv, acc = carry
        acc = jnp.where(lane == sec, inv, acc)
        h = advance(hx[half, :], 0.5 * params[sec, 0], params[sec, 1], inv).astype(F32)
        hx[half, :] = h
        return inverse(h), acc

    inv, acc = lax.fori_loop(
        0, SECTIONS - 1, scale_step, (inverse(hx[half, :]), jnp.zeros((OWN, 128), F32))
    )
    tile[...] = jnp.where(lane == SECTIONS - 1, inv, acc)
    sc1[s] = tile[...]
    for i, peer in enumerate(seg_peers):
        post(remote(tile, sc1.at[s], r1_send.at[i], r1_recv.at[s], device_id=at(peer, d)))

    def spread(sec, _):
        mine = pl.ds(pl.multiple_of(d * IN, IN), IN)
        loss_cols = pl.ds(pl.multiple_of(s * OUT, OUT), OUT)
        gain_b[sec] = jnp.broadcast_to(0.5 * params[sec, 0, :, mine], (8, IN))
        mix_b[sec] = jnp.broadcast_to(params[sec, 1, :, mine], (8, IN))
        gain_u[sec] = jnp.broadcast_to(0.5 * params[sec, 0, :, loss_cols], (8, OUT))
        mix_u[sec] = jnp.broadcast_to(params[sec, 1, :, loss_cols], (8, OUT))
        return 0

    lax.fori_loop(0, SECTIONS, spread, 0)
    for i, peer in enumerate(seg_peers):
        remote(tile, sc1.at[peer], r1_send.at[i], r1_recv.at[peer], device_id=at(peer, d)).wait_recv()
    inv_own[...] = sc1[...].reshape(TOK, 128)
    packed[...] = inv_own[...].T[0:SECTIONS, :]

    def r2_copy(i):
        peer = lax.rem(d + i, DP)
        return remote(packed, sc2.at[d], r2_send.at[i], r2_recv.at[d], device_id=at(s, peer))

    @pl.when(home)
    def _():
        for i in range(1, DP):
            r2_copy(i).start()
        sc2[d] = packed[...]

    for copy in w_copies:
        copy.wait()

    first, second = pl.ds(0, HALF), pl.ds(HALF, HALF)

    def replica_of(parity, n):
        return lax.rem(y + n, 4) * 2 + parity

    def a1_copy(to_y):
        j = to_y * 2 + 1 - zh
        return remote(
            stage.at[j, :, first], in_a1.at[to_y], a1_send.at[to_y], a1_recv.at[to_y], device_id=at(s, pair)
        )

    def b1_copy(to_y, z):
        j = to_y * 2 + z
        return remote(
            stage.at[j, :, second], in_b1.at[y * 2 + z], b1_send.at[j], b1_recv.at[y * 2 + z],
            device_id=at(s, to_y * 2 + zh),
        )

    def a2_copy(to_y):
        return remote(
            out_a2.at[to_y], in_a2.at[y], a2_send.at[to_y], a2_recv.at[y], device_id=at(s, to_y * 2 + zh)
        )

    def b2_copy():
        return remote(out_b2, in_b2, b2_send.at[0], b2_recv.at[0], device_id=at(s, pair))

    def join(j, z):
        to_y = j // 2
        rows = pl.ds(pl.multiple_of(j * TOK, TOK), TOK)
        part = jnp.dot(feat[rows, :], w[...], preferred_element_type=F32)
        stage[j] = part.astype(BF16)

        @pl.when(z == zh)
        def _():
            keep_a[to_y] = part[:, 0:HALF]

        @pl.when(z != zh)
        def _():
            a1_copy(to_y).start()

        @pl.when(to_y == y)
        def _():
            keep_b[z] = part[:, HALF:OUT]

        @pl.when(to_y != y)
        def _():
            b1_copy(to_y, z).start()

    def f_copy(j):
        rows = pl.ds(pl.multiple_of(j * TOK, TOK), TOK)
        return remote(feat.at[rows], feat.at[rows], f_send.at[j // 2], f_recv.at[j // 2], device_id=at(sib, d))

    def work(n, _):
        j = replica_of(c, n)
        slot = j // 2
        remote(
            stream.at[:, pl.ds(0, IN)], h0.at[slot], h_send.at[0], h_recv.at[slot], device_id=at(sib, d)
        ).wait_recv()

        @pl.when(j != d)
        def _():
            remote(packed, sc2.at[j], r2_send.at[0], r2_recv.at[j], device_id=at(s, j)).wait_recv()

        inv_j[...] = jnp.concatenate([sc2[j], jnp.zeros((128 - SECTIONS, 128), F32)], 0).T

        def one(t, _):
            r = pl.multiple_of((t // 2) * 32, 32)
            col = pl.multiple_of((t % 2) * 512, 512)
            cols = pl.ds(col, 512)
            taps = run_sections(
                h0[slot, pl.ds(r, 32), cols].astype(F32), inv_j[pl.ds(r, 32), :],
                lambda sec: gain_b[sec, :, cols], lambda sec: mix_b[sec, :, cols],
            )
            for i, tap in enumerate(taps):
                feat[pl.ds(pl.multiple_of(j * TOK + r, 32), 32), pl.ds(pl.multiple_of(i * IN + col, 512), 512)] = tap
            return 0

        lax.fori_loop(0, 8, one, 0)
        f_copy(j).start()
        join(j, c)
        return 0

    lax.fori_loop(1, 5, work, 0)

    def other(n, _):
        j = replica_of(1 - c, n)
        f_copy(j).wait_recv()
        join(j, 1 - c)
        return 0

    lax.fori_loop(1, 5, other, 0)

    up_copy.wait()

    def up_one(t, _):
        rows = pl.ds(pl.multiple_of(t * 32, 32), 32)
        taps = run_sections(
            up_in[rows, :].astype(F32), inv_own[rows, :], lambda sec: gain_u[sec], lambda sec: mix_u[sec]
        )
        upper[rows, :] = taps[2].astype(F32)
        return 0

    lax.fori_loop(0, 4, up_one, 0)

    for i in range(1, 5):
        to_y = lax.rem(y + i, 4)
        remote(
            stage.at[0, :, first], in_a1.at[to_y], a1_send.at[to_y], a1_recv.at[to_y], device_id=at(s, pair)
        ).wait_recv()
        total = keep_a[to_y] + in_a1[to_y].astype(F32)
        if i < 4:
            out_a2[to_y] = total.astype(BF16)
            post(a2_copy(to_y))
        else:
            own[:, 0:HALF] = total

    for step in range(2):
        z = 1 - zh if step == 0 else zh
        total = keep_b[z]
        for from_y in y_peers:
            slot = from_y * 2 + z
            remote(
                stage.at[0, :, second], in_b1.at[slot], b1_send.at[slot], b1_recv.at[slot],
                device_id=at(s, from_y * 2 + zh),
            ).wait_recv()
            total = total + in_b1[slot].astype(F32)
        if step == 0:
            out_b2[...] = total.astype(BF16)
            post(b2_copy())
        else:
            own[:, HALF:OUT] = total

    def turn(t, _):
        rows = pl.ds(pl.multiple_of((t % 8) * TOK, TOK), TOK)
        cols = pl.ds(pl.multiple_of((t // 8) * 512, 512), 512)
        feat_t[cols, rows] = feat[rows, cols].T
        return 0

    lax.fori_loop(0, 48, turn, 0)

    inv_count = []
    for k in range(1, STEPS + 1):
        count = jnp.int32(0)
        for m in range(NMB):
            count = count + jnp.maximum(lengths[0, m] - k, 0)
        inv_count.append(1.0 / (jnp.full((1, 128), jnp.maximum(count, 1), jnp.int32).astype(F32) * D))

    here = pl.ds(pl.multiple_of(d * TOK, TOK), TOK)

    def draft(q, _):
        cols = pl.ds(pl.multiple_of(q * 128, 128), 128)
        joined = own[:, cols]
        up = upper[:, cols]
        dec = decay[:, cols]
        plen = left[...]

        def carry_of(k):
            return dec * mask_t[:, k - 1:k]

        state = joined
        pulls = []
        for k in range(1, STEPS + 1):
            state = joined + carry_of(k) * pltpu.roll(state, 1, 0)
            target = pltpu.roll(up, TOK - k, 0)
            diff = jnp.where(plen > k, state - target, 0.0)
            loss_acc[k - 1] += jnp.sum((diff * diff).reshape(TOK // 8, 8, 128), axis=0)
            pulls.append(diff * (2.0 * inv_count[k - 1]))
        back = pulls[STEPS - 1]
        total = back
        for k in range(STEPS - 1, 0, -1):
            back = pulls[k - 1] + pltpu.roll(carry_of(k + 1) * back, TOK - 1, 0)
            total = total + back
        total = total + pltpu.roll(carry_of(1) * back, TOK - 1, 0)
        rows_all[here, cols] = total.astype(BF16)
        return 0

    def rows_of(j):
        return pl.ds(pl.multiple_of(j * TOK, TOK), TOK)

    def q_copy(part, i, source, peer):
        block = rows_all.at[rows_of(source), first if part == 0 else second]
        return remote(block, block, q_send.at[part * 4 + i], q_recv.at[part * DP + source], device_id=at(s, peer))

    def qa_copy(i, from_y, to_y):
        block = rows_all.at[rows_of(from_y * 2 + 1 - zh), first]
        return remote(block, block, qa_send.at[i], qa_recv.at[from_y], device_id=at(s, to_y * 2 + zh))

    def qb_copy(i, from_y, z):
        block = rows_all.at[rows_of(from_y * 2 + z), second]
        return remote(block, block, qb_send.at[i], qb_recv.at[from_y], device_id=at(s, pair))

    for i, from_y in enumerate(y_peers):
        remote(
            out_a2.at[0], in_a2.at[from_y], a2_send.at[0], a2_recv.at[from_y], device_id=at(s, from_y * 2 + zh)
        ).wait_recv()
        own[:, 0:HALF] += in_a2[from_y].astype(F32)
    lax.fori_loop(0, 2, draft, 0)
    for i, peer in enumerate([pair] + [p * 2 + zh for p in y_peers]):
        post(q_copy(0, i, d, peer))
    b2_copy().wait_recv()
    own[:, HALF:OUT] += in_b2[...].astype(F32)
    lax.fori_loop(2, 4, draft, 0)
    for i, peer in enumerate([pair] + [p * 2 + zh for p in y_peers]):
        post(q_copy(1, i, d, peer))

    q_copy(0, 0, pair, pair).wait_recv()
    for i, to_y in enumerate(y_peers):
        post(qa_copy(i, y, to_y))

    lane = lax.broadcasted_iota(jnp.int32, (8, 128), 1)
    losses = jnp.zeros((8, 128), F32)
    for k in range(1, STEPS + 1):
        losses = jnp.where(lane == k - 1, jnp.sum(loss_acc[k - 1]) * inv_count[k - 1], losses)
    loss_tile[...] = losses
    loss_all[s] = losses
    for i, peer in enumerate(seg_peers):
        post(remote(loss_tile, loss_all.at[s], l_send.at[i], l_recv.at[s], device_id=at(peer, d)))

    for i, from_y in enumerate(y_peers):
        q_copy(1, 0, from_y * 2 + zh, pair).wait_recv()
        post(qb_copy(i, from_y, zh))

    for i, peer in enumerate(seg_peers):
        remote(loss_tile, loss_all.at[peer], l_send.at[i], l_recv.at[peer], device_id=at(peer, d)).wait_recv()
    summed = loss_all[0]
    for i in range(1, SEG):
        summed = summed + loss_all[i]
    loss_out[...] = summed

    q_copy(1, 0, pair, pair).wait_recv()
    for from_y in y_peers:
        q_copy(0, 0, from_y * 2 + zh, pair).wait_recv()
        qa_copy(0, from_y, from_y).wait_recv()
        qb_copy(0, from_y, 1 - zh).wait_recv()
    rows_copy = pltpu.make_async_copy(rows_all, rows_out, in_sem.at[0])
    rows_copy.start()

    for copy in sends:
        copy.wait_send()

    @pl.when(home)
    def _():
        for i in range(1, DP):
            h_copy(i).wait_send()
            r2_copy(i).wait_send()

    for n in range(1, 5):
        f_copy(replica_of(c, n)).wait_send()
    for to_y in range(4):
        a1_copy(to_y).wait_send()
    for to_y in y_peers:
        for z in range(2):
            b1_copy(to_y, z).wait_send()
    rows_copy.wait()


def gradient(feat_t, rows, loss, grad_out, loss_out, grad, sem):
    def out_copy(t):
        return pltpu.make_async_copy(
            grad.at[t], grad_out.at[pl.ds(pl.multiple_of(t * 256, 256), 256)], sem.at[t]
        )

    def one(t, _):
        block = pl.ds(pl.multiple_of(t * 256, 256), 256)
        grad[t] = jnp.dot(feat_t[block, :], rows[...], preferred_element_type=F32)
        out_copy(t).start()
        return 0

    lax.fori_loop(0, 12, one, 0)
    loss_out[...] = loss[0:1, 0:STEPS]
    for t in range(12):
        out_copy(t).wait()


def local(stream_in, sec_gain, sec_mix, fc_weight, decay, lengths, ttt_mask):
    vmem = pltpu.VMEM
    dma = pltpu.SemaphoreType.DMA
    scratch = [
        vmem((1, OUT), F32), pltpu.SMEM((1, NMB), jnp.int32), vmem((STEPS, TOK), jnp.int32),
        vmem((SECTIONS, 2, 1, D), F32),
        vmem((SECTIONS, 8, IN), F32), vmem((SECTIONS, 8, IN), F32),
        vmem((SECTIONS, 8, OUT), F32), vmem((SECTIONS, 8, OUT), F32),
        vmem((16, D), BF16), vmem((16, D), F32),
        vmem((4, TOK, IN), BF16),
        vmem((OWN, 128), F32), vmem((SEG, OWN, 128), F32),
        vmem((SECTIONS, 128), F32), vmem((DP, SECTIONS, 128), F32),
        vmem((TOK, 128), F32), vmem((TOK, 128), F32),
        vmem((3 * IN, OUT), BF16),
        vmem((DP * TOK, 3 * IN), BF16),
        vmem((DP, TOK, OUT), BF16), vmem((4, TOK, HALF), F32), vmem((2, TOK, HALF), F32),
        vmem((4, TOK, HALF), BF16), vmem((DP, TOK, HALF), BF16),
        vmem((4, TOK, HALF), BF16), vmem((4, TOK, HALF), BF16),
        vmem((TOK, HALF), BF16), vmem((TOK, HALF), BF16), vmem((TOK, OUT), F32),
        vmem((TOK, OUT), BF16), vmem((TOK, OUT), F32),
        vmem((TOK, 128), F32), vmem((TOK, 128), F32), vmem((TOK, 128), jnp.int32),
        vmem((STEPS, 8, 128), F32), vmem((8, 128), F32), vmem((SEG, 8, 128), F32),
        vmem((DP * TOK, OUT), BF16),
        dma((10,)), dma((5,)), dma((SEG,)), dma((10,)), dma((DP,)), dma((4,)),
        dma((SEG,)), dma((SEG,)), dma((DP,)), dma((DP,)), dma((4,)), dma((4,)),
        dma((4,)), dma((4,)), dma((DP,)), dma((DP,)), dma((4,)), dma((4,)), dma((1,)), dma((1,)),
        dma((8,)), dma((2 * DP,)), dma((3,)), dma((4,)), dma((3,)), dma((4,)), dma((SEG,)), dma((SEG,)),
    ]
    any_space = pl.BlockSpec(memory_space=pl.ANY)
    in_hbm = pl.BlockSpec(memory_space=pltpu.HBM)
    in_vmem = pl.BlockSpec(memory_space=pltpu.VMEM)
    loss, feat_t, rows = pl.pallas_call(
        kernel,
        out_shape=(
            jax.ShapeDtypeStruct((8, 128), F32),
            jax.ShapeDtypeStruct((3 * IN, DP * TOK), BF16),
            jax.ShapeDtypeStruct((DP * TOK, OUT), BF16),
        ),
        in_specs=[in_hbm] * 7,
        out_specs=(in_vmem, in_vmem, any_space),
        scratch_shapes=scratch,
        compiler_params=pltpu.CompilerParams(
            collective_id=0, has_side_effects=True, vmem_limit_bytes=VM1 * 1024 * 1024
        ),
        name="window",
    )(stream_in, sec_gain, sec_mix, fc_weight, decay.reshape(1, OUT), lengths, ttt_mask)
    grad, step_loss = pl.pallas_call(
        gradient,
        out_shape=(
            jax.ShapeDtypeStruct((3 * IN, OUT), F32),
            jax.ShapeDtypeStruct((1, STEPS), F32),
        ),
        in_specs=[in_vmem] * 3,
        out_specs=(any_space, in_vmem),
        scratch_shapes=[vmem((12, 256, OUT), F32), dma((12,))],
        compiler_params=pltpu.CompilerParams(vmem_limit_bytes=VM2 * 1024 * 1024),
        name="gradient",
    )(feat_t, rows, loss)
    return step_loss, grad.reshape(3, IN, OUT)


def solution(mesh):
    in_specs = (
        P("dp", None),
        P("segment", None),
        P("segment", None),
        P(None, "dp", "segment"),
        P("segment"),
        P("dp", None),
        P(None, "dp"),
    )
    out_specs = (P("dp", None), P(None, "dp", "segment"))
    return jax.shard_map(local, mesh=mesh, in_specs=in_specs, out_specs=out_specs, check_vma=False)
```

time: 94.5 us -> 92.6 us (0.980)
  Pallas kernels: 84.9 us -> 83.6 us
    pallas_call x1, Pallas kernels: 84.9 us -> 76.9 us  [local(): pl.pallas_call(kernel, out_shape=(jax.ShapeDtypeStruct((8, 128), F32), ja...]
    pallas_call x0 -> x1, Pallas kernels: none -> 6.65 us  [local(): pl.pallas_call(gradient, out_shape=(jax.ShapeDtypeStruct((3 * IN, OUT), F...]
    slice x1 -> x0, local copies, waits for them, and re-layouts: 1.18 us -> none  [local(): return (loss[0:1, 0:STEPS], grad)]
    unnamed x1 -> x14, local copies, waits for them, and re-layouts: 6.2 us -> 7.01 us
where the time goes in v3:
time: 92.6 us; the launch traced here: 91.2 us
  Pallas kernels  83.6 us (90%)
  local copies, waits for them, and re-layouts  7.01 us (8%)
    pallas_call x1, Pallas kernels, local(): pl.pallas_call(kernel, out_shape=(jax.ShapeDtypeStruct((8, 128), F32), ja...  76.9 us
    unnamed x14, local copies, waits for them, and re-layouts  7.01 us
    pallas_call x1, Pallas kernels, local(): pl.pallas_call(gradient, out_shape=(jax.ShapeDtypeStruct((3 * IN, OUT), F...  6.65 us

profile of v3, /device:TPU:1, one launch (start us, length us, event | category | flops | bytes accessed | tf_op | source)
XLA Modules:
  0.0 91.2 jit_solution(4256343242854883910)
XLA Ops:
  0.6 0.0 copy-start
  0.6 1.9 %copy-done = bf16[3,1024,512]{2,1,0:T(8,128)(2,1)S(1)} copy-done((bf16[3,1024,512]{2,1,0:T(8,128)(2,1)S(1)}, bf16[3,1024,512]{2,1,0:T(8,128)(2,1)}, u32[]{:S(2)}) %copy-start) | copy-done | bytes 3145752
  2.5 0.0 copy-start.1
  2.5 1.6 %copy-done.1 = bf16[128,8192]{1,0:T(8,128)(2,1)S(1)} copy-done((bf16[128,8192]{1,0:T(8,128)(2,1)S(1)}, bf16[128,8192]{1,0:T(8,128)(2,1)}, u32[]{:S(2)}) %copy-start.1) | copy-done | bytes 2097176
  4.1 0.0 copy-start.2
  4.1 0.8 copy-done.2
  4.9 0.0 copy-start.3
  4.9 0.8 copy-done.3
  5.6 0.0 copy-start.4
  5.6 0.7 copy-done.4
  6.3 0.0 copy-start.5
  6.3 0.7 copy-done.5
  7.0 0.0 copy-start.6
  7.0 0.7 copy-done.6
  7.7 76.9 %window.1 = (f32[8,128]{1,0:T(8,128)S(1)}, bf16[3072,1024]{1,0:T(8,128)(2,1)S(1)}, bf16[1024,512]{1,0:T(8,128)(2,1)S(1)}) custom-call(bf16[128,8192]{1,0:T(8,128)(2,1)S(1)} %copy-done.1, f32[1,8192]{1,0:T(1,128)S(1)} %copy-done.2, f32[1,8192]{1,0:T(1,128)S(1)} %copy-done.3, bf16[3,1024,512]{2,1,0:T(8,128)(2,1)S(1)} %copy-done, f32[1,512]{1,0:T(1,128)S(1)} %bitcast.2, ...), custom_call_target="tpu_custom_call" | custom-call | tf_op jit(solution)/shard_map/window/pallas_call | solution.py:522
  84.6 6.6 %gradient.1 = (f32[3072,512]{1,0:T(8,128)}, f32[1,7]{1,0:T(1,128)}) custom-call(bf16[3072,1024]{1,0:T(8,128)(2,1)S(1)} %get-tuple-element.7.feat_t, bf16[1024,512]{1,0:T(8,128)(2,1)S(1)} %get-tuple-element.8.rows, f32[8,128]{1,0:T(8,128)S(1)} %get-tuple-element.9.loss), custom_call_target="tpu_custom_call" | custom-call | tf_op jit(solution)/shard_map/gradient/pallas_call | solution.py:537
Async XLA Ops:
  0.6 1.9 %copy-start = (bf16[3,1024,512]{2,1,0:T(8,128)(2,1)S(1)}, bf16[3,1024,512]{2,1,0:T(8,128)(2,1)}, u32[]{:S(2)}) copy-start(bf16[3,1024,512]{2,1,0:T(8,128)(2,1)} %weight.1) | copy-start | bytes 9437188
  2.5 1.6 %copy-start.1 = (bf16[128,8192]{1,0:T(8,128)(2,1)S(1)}, bf16[128,8192]{1,0:T(8,128)(2,1)}, u32[]{:S(2)}) copy-start(bf16[128,8192]{1,0:T(8,128)(2,1)} %stream.1) | copy-start | bytes 6291460
  4.1 0.8 copy-start.2
  4.9 0.8 copy-start.3
  5.6 0.7 copy-start.4
  6.3 0.7 copy-start.5
  7.0 0.7 copy-start.6

commit v4 on v3

--- a/solution.py
+++ b/solution.py
@@ -16,8 +16,8 @@
 TOK = 128
 SEG = 16
 DP = 8
-VM1 = 40
-VM2 = 32
+VM1 = 56
+VM2 = 56
 IN = D // DP
 OUT = D // SEG
 OWN = TOK // SEG
@@ -36,26 +36,26 @@
     return (h + (mix * u) * (1.0 + jnp.tanh(u))).astype(BF16)
 
 
-def run_sections(h, inv_cols, gain_of, mix_of):
-    rows = h.shape[0]
+def run_sections(h, inv_of, gain_of, mix_of):
+    rows, cols = h.shape
     taps = []
     for sec in range(SECTIONS):
         gain = jnp.concatenate([gain_of(sec)] * (rows // 8), 0)
         mix = jnp.concatenate([mix_of(sec)] * (rows // 8), 0)
-        out = advance(h, gain, mix, inv_cols[:, sec:sec + 1])
+        out = advance(h, gain, mix, jnp.concatenate([inv_of(sec)] * (cols // 128), 1))
         if sec in TAPS:
             taps.append(out)
         h = out.astype(F32)
     return taps
 
 
-def kernel(stream, gain, mix, weight, decay_in, lengths_in, mask_in, loss_out, feat_t, rows_out,
-           decay, lengths, mask, params, gain_b, mix_b, gain_u, mix_u, rows16, hx, h0, tile, sc1, packed, sc2, inv_own, inv_j,
-           w, feat, stage, keep_a, keep_b, in_a1, in_b1, out_a2, in_a2, out_b2, in_b2, own,
+def kernel(stream, gain, mix, weight, decay_in, lengths_in, mask_in, loss_out, feat_out, rows_out,
+           decay, lengths, mask, params, gain_b, mix_b, gain_u, mix_u, rows16, hx, h0, tile, sc1, packed, sc2, inv_own, inv_b,
+           w, feat, feat_t, stage, keep_a, keep_b, in_a1, in_b1, out_a2, in_a2, out_b2, in_b2, own,
            up_in, upper, mask_t, mask_pad, left, loss_acc, loss_tile, loss_all, rows_all,
            in_sem, g_send, g_recv, gf_send, h_send, h_recv, r1_send, r1_recv, r2_send, r2_recv, f_send, f_recv,
            a1_send, a1_recv, b1_send, b1_recv, a2_send, a2_recv, b2_send, b2_recv,
-           q_send, q_recv, qa_send, qa_recv, qb_send, qb_recv, l_send, l_recv):
+           q_send, q_recv, qa_send, qa_recv, qb_send, qb_recv, l_send, l_recv, o_sem):
     s = lax.axis_index("segment")
     d = lax.axis_index("dp")
     c = lax.rem(s, 2)
@@ -65,11 +65,12 @@
     sib = s + 1 - 2 * c
     home = zh == c
     seg_peers = [lax.rem(s + i, SEG) for i in range(1, SEG)]
-    dp_peers = [lax.rem(d + i, DP) for i in range(1, DP)]
     y_peers = [lax.rem(y + i, 4) for i in range(1, 4)]
     plane = (s // 8) * 8
     x_peers = [plane + lax.rem(s - plane + 2 * i, 8) for i in range(1, 4)]
     across = lax.rem(s + 8, SEG)
+    far = [(s, p * 2 + zh) for p in y_peers]
+    far = [(across, lax.rem(y + i, 4) * 2 + 1 - zh) for i in (2, 1, 3, 0)] + far
     remote = functools.partial(pltpu.make_async_remote_copy, device_id_type=MESH)
 
     gain_copy = pltpu.make_async_copy(gain, params.at[s, 0], in_sem.at[5])
@@ -95,11 +96,11 @@
     barrier = pltpu.get_barrier_semaphore()
     for peer in seg_peers:
         pl.semaphore_signal(barrier, inc=1, device_id=at(peer, d), device_id_type=MESH)
-    for peer in dp_peers:
-        pl.semaphore_signal(barrier, inc=1, device_id=at(s, peer), device_id_type=MESH)
+    for seg, peer in far + [(s, pair)]:
+        pl.semaphore_signal(barrier, inc=1, device_id=at(seg, peer), device_id_type=MESH)
     gain_copy.wait()
     mix_copy.wait()
-    pl.semaphore_wait(barrier, SEG - 1 + DP - 1)
+    pl.semaphore_wait(barrier, SEG - 1 + DP)
 
     def g_copy(slot, peer, send):
         return remote(params.at[slot], params.at[slot], send, g_recv.at[slot], device_id=at(peer, d))
@@ -114,18 +115,18 @@
         post(g_copy(s, peer, g_send.at[i]))
 
     def h_copy(i):
-        peer = lax.rem(d + i, DP)
+        seg, peer = far[i]
         return remote(
-            stream.at[:, pl.ds(pl.multiple_of(peer * IN, IN), IN)], h0.at[d // 2],
-            h_send.at[i], h_recv.at[d // 2], device_id=at(s, peer),
+            stream.at[:, pl.ds(pl.multiple_of(peer * IN, IN), IN)], h0.at[y],
+            h_send.at[i], h_recv.at[y], device_id=at(seg, peer),
         )
 
     @pl.when(home)
     def _():
-        for i in range(1, DP):
+        for i in range(DP - 1):
             h_copy(i).start()
         pltpu.make_async_copy(
-            stream.at[:, pl.ds(pl.multiple_of(d * IN, IN), IN)], h0.at[d // 2], h_recv.at[d // 2]
+            stream.at[:, pl.ds(pl.multiple_of(d * IN, IN), IN)], h0.at[y], h_recv.at[y]
         ).start()
 
     up_copy.start()
@@ -183,7 +184,8 @@
     )
     tile[...] = jnp.where(lane == SECTIONS - 1, inv, acc)
     sc1[s] = tile[...]
-    for i, peer in enumerate(seg_peers):
+    chips = [lax.rem(s // 2 + i, SEG // 2) * 2 for i in range(1, SEG // 2)]
+    for i, peer in enumerate([p + zh for p in chips] + [sib] + [p + 1 - zh for p in chips]):
         post(remote(tile, sc1.at[s], r1_send.at[i], r1_recv.at[s], device_id=at(peer, d)))
 
     def spread(sec, _):
@@ -202,14 +204,36 @@
     packed[...] = inv_own[...].T[0:SECTIONS, :]
 
     def r2_copy(i):
-        peer = lax.rem(d + i, DP)
-        return remote(packed, sc2.at[d], r2_send.at[i], r2_recv.at[d], device_id=at(s, peer))
+        seg, peer = far[i]
+        return remote(packed, sc2.at[d], r2_send.at[i], r2_recv.at[d], device_id=at(seg, peer))
 
     @pl.when(home)
     def _():
-        for i in range(1, DP):
+        for i in range(DP - 1):
             r2_copy(i).start()
         sc2[d] = packed[...]
+
+    up_copy.wait()
+
+    def spread_rows(inv):
+        for sec in range(SECTIONS):
+            inv_b[sec] = jnp.broadcast_to(inv[:, sec:sec + 1], (TOK, 128))
+
+    def find_upper():
+        spread_rows(inv_own[...])
+
+        def up_one(t, _):
+            rows = pl.ds(pl.multiple_of(t * 32, 32), 32)
+            taps = run_sections(
+                up_in[rows, :].astype(F32), lambda sec: inv_b[sec, rows, :],
+                lambda sec: gain_u[sec], lambda sec: mix_u[sec],
+            )
+            upper[rows, :] = taps[2].astype(F32)
+            return 0
+
+        lax.fori_loop(0, 4, up_one, 0)
+
+    pl.when(jnp.logical_not(home))(find_upper)
 
     for copy in w_copies:
         copy.wait()
@@ -262,9 +286,16 @@
         def _():
             b1_copy(to_y, z).start()
 
-    def f_copy(j):
-        rows = pl.ds(pl.multiple_of(j * TOK, TOK), TOK)
-        return remote(feat.at[rows], feat.at[rows], f_send.at[j // 2], f_recv.at[j // 2], device_id=at(sib, d))
+    def f_copy(j, part):
+        rows = pl.ds(pl.multiple_of(j * TOK + part * 64, 64), 64)
+        slot = (j // 2) * 2 + part
+        return remote(feat.at[rows], feat.at[rows], f_send.at[slot], f_recv.at[slot], device_id=at(sib, d))
+
+    def join_other(n):
+        j = replica_of(1 - c, n)
+        f_copy(j, 0).wait_recv()
+        f_copy(j, 1).wait_recv()
+        join(j, 1 - c)
 
     def work(n, _):
         j = replica_of(c, n)
@@ -275,56 +306,64 @@
 
         @pl.when(j != d)
         def _():
-            remote(packed, sc2.at[j], r2_send.at[0], r2_recv.at[j], device_id=at(s, j)).wait_recv()
-
-        inv_j[...] = jnp.concatenate([sc2[j], jnp.zeros((128 - SECTIONS, 128), F32)], 0).T
+            remote(packed, sc2.at[j], r2_send.at[0], r2_recv.at[j], device_id=at(sib, d)).wait_recv()
+
+        spread_rows(jnp.concatenate([sc2[j], jnp.zeros((128 - SECTIONS, 128), F32)], 0).T)
 
         def one(t, _):
-            r = pl.multiple_of((t // 2) * 32, 32)
-            col = pl.multiple_of((t % 2) * 512, 512)
-            cols = pl.ds(col, 512)
+            rows = pl.ds(pl.multiple_of(t * 16, 16), 16)
             taps = run_sections(
-                h0[slot, pl.ds(r, 32), cols].astype(F32), inv_j[pl.ds(r, 32), :],
-                lambda sec: gain_b[sec, :, cols], lambda sec: mix_b[sec, :, cols],
+                h0[slot, rows, :].astype(F32), lambda sec: inv_b[sec, rows, :],
+                lambda sec: gain_b[sec], lambda sec: mix_b[sec],
             )
             for i, tap in enumerate(taps):
-                feat[pl.ds(pl.multiple_of(j * TOK + r, 32), 32), pl.ds(pl.multiple_of(i * IN + col, 512), 512)] = tap
+                feat[pl.ds(pl.multiple_of(j * TOK + t * 16, 16), 16), i * IN:(i + 1) * IN] = tap
             return 0
 
-        lax.fori_loop(0, 8, one, 0)
-        f_copy(j).start()
+        lax.fori_loop(0, 4, one, 0)
+        f_copy(j, 0).start()
+        lax.fori_loop(4, 8, one, 0)
+        f_copy(j, 1).start()
         join(j, c)
+
+        @pl.when(n > 0)
+        def _():
+            join_other(n - 1)
+
         return 0
 
-    lax.fori_loop(1, 5, work, 0)
-
-    def other(n, _):
-        j = replica_of(1 - c, n)
-        f_copy(j).wait_recv()
-        join(j, 1 - c)
+    lax.fori_loop(0, 4, work, 0)
+    join_other(3)
+
+    pl.when(home)(find_upper)
+
+    def turn_out(t):
+        rows = pl.ds(pl.multiple_of(t * 512, 512), 512)
+        return pltpu.make_async_copy(feat_t.at[rows], feat_out.at[rows], o_sem.at[t])
+
+    def turn(t, _):
+        cols = pl.ds(pl.multiple_of(t * 512, 512), 512)
+
+        def block(j, _):
+            rows = pl.ds(pl.multiple_of(j * TOK, TOK), TOK)
+            feat_t[cols, rows] = feat[rows, cols].T
+            return 0
+
+        lax.fori_loop(0, 8, block, 0)
+        turn_out(t).start()
         return 0
 
-    lax.fori_loop(1, 5, other, 0)
-
-    up_copy.wait()
-
-    def up_one(t, _):
-        rows = pl.ds(pl.multiple_of(t * 32, 32), 32)
-        taps = run_sections(
-            up_in[rows, :].astype(F32), inv_own[rows, :], lambda sec: gain_u[sec], lambda sec: mix_u[sec]
-        )
-        upper[rows, :] = taps[2].astype(F32)
-        return 0
-
-    lax.fori_loop(0, 4, up_one, 0)
-
-    for i in range(1, 5):
+    @pl.when(jnp.logical_not(home))
+    def _():
+        lax.fori_loop(0, 2, turn, 0)
+
+    for i in (1, 2, 3, 0):
         to_y = lax.rem(y + i, 4)
         remote(
             stage.at[0, :, first], in_a1.at[to_y], a1_send.at[to_y], a1_recv.at[to_y], device_id=at(s, pair)
         ).wait_recv()
         total = keep_a[to_y] + in_a1[to_y].astype(F32)
-        if i < 4:
+        if i > 0:
             out_a2[to_y] = total.astype(BF16)
             post(a2_copy(to_y))
         else:
@@ -346,13 +385,11 @@
         else:
             own[:, HALF:OUT] = total
 
-    def turn(t, _):
-        rows = pl.ds(pl.multiple_of((t % 8) * TOK, TOK), TOK)
-        cols = pl.ds(pl.multiple_of((t // 8) * 512, 512), 512)
-        feat_t[cols, rows] = feat[rows, cols].T
-        return 0
-
-    lax.fori_loop(0, 48, turn, 0)
+    @pl.when(home)
+    def _():
+        lax.fori_loop(0, 2, turn, 0)
+
+    lax.fori_loop(2, 4, turn, 0)
 
     inv_count = []
     for k in range(1, STEPS + 1):
@@ -419,9 +456,15 @@
     for i, peer in enumerate([pair] + [p * 2 + zh for p in y_peers]):
         post(q_copy(1, i, d, peer))
 
+    lax.fori_loop(4, 5, turn, 0)
     q_copy(0, 0, pair, pair).wait_recv()
     for i, to_y in enumerate(y_peers):
         post(qa_copy(i, y, to_y))
+
+    lax.fori_loop(5, 6, turn, 0)
+    for i, from_y in enumerate(y_peers):
+        q_copy(1, 0, from_y * 2 + zh, pair).wait_recv()
+        post(qb_copy(i, from_y, zh))
 
     lane = lax.broadcasted_iota(jnp.int32, (8, 128), 1)
     losses = jnp.zeros((8, 128), F32)
@@ -432,10 +475,6 @@
     for i, peer in enumerate(seg_peers):
         post(remote(loss_tile, loss_all.at[s], l_send.at[i], l_recv.at[s], device_id=at(peer, d)))
 
-    for i, from_y in enumerate(y_peers):
-        q_copy(1, 0, from_y * 2 + zh, pair).wait_recv()
-        post(qb_copy(i, from_y, zh))
-
     for i, peer in enumerate(seg_peers):
         remote(loss_tile, loss_all.at[peer], l_send.at[i], l_recv.at[peer], device_id=at(peer, d)).wait_recv()
     summed = loss_all[0]
@@ -456,35 +495,51 @@
 
     @pl.when(home)
     def _():
-        for i in range(1, DP):
+        for i in range(DP - 1):
             h_copy(i).wait_send()
             r2_copy(i).wait_send()
 
-    for n in range(1, 5):
-        f_copy(replica_of(c, n)).wait_send()
+    for n in range(4):
+        for part in range(2):
+            f_copy(replica_of(c, n), part).wait_send()
     for to_y in range(4):
         a1_copy(to_y).wait_send()
     for to_y in y_peers:
         for z in range(2):
             b1_copy(to_y, z).wait_send()
+    for t in range(6):
+        turn_out(t).wait()
     rows_copy.wait()
 
 
-def gradient(feat_t, rows, loss, grad_out, loss_out, grad, sem):
+def gradient(feat_in, rows_in, loss_in, grad_out, loss_out, feat_t, rows, loss, grad, i_sem, sem):
+    def block(t):
+        return pl.ds(pl.multiple_of(t * 512, 512), 512)
+
+    def in_copy(t):
+        return pltpu.make_async_copy(feat_in.at[block(t)], feat_t.at[block(t)], i_sem.at[t])
+
     def out_copy(t):
-        return pltpu.make_async_copy(
-            grad.at[t], grad_out.at[pl.ds(pl.multiple_of(t * 256, 256), 256)], sem.at[t]
-        )
+        return pltpu.make_async_copy(grad.at[t], grad_out.at[block(t)], sem.at[t])
+
+    rows_copy = pltpu.make_async_copy(rows_in, rows, i_sem.at[6])
+    loss_copy = pltpu.make_async_copy(loss_in, loss, i_sem.at[7])
+    rows_copy.start()
+    for t in range(6):
+        in_copy(t).start()
+    loss_copy.start()
+    rows_copy.wait()
 
     def one(t, _):
-        block = pl.ds(pl.multiple_of(t * 256, 256), 256)
-        grad[t] = jnp.dot(feat_t[block, :], rows[...], preferred_element_type=F32)
+        in_copy(t).wait()
+        grad[t] = jnp.dot(feat_t[block(t), :], rows[...], preferred_element_type=F32)
         out_copy(t).start()
         return 0
 
-    lax.fori_loop(0, 12, one, 0)
+    lax.fori_loop(0, 6, one, 0)
+    loss_copy.wait()
     loss_out[...] = loss[0:1, 0:STEPS]
-    for t in range(12):
+    for t in range(6):
         out_copy(t).wait()
 
 
@@ -500,9 +555,9 @@
         vmem((4, TOK, IN), BF16),
         vmem((OWN, 128), F32), vmem((SEG, OWN, 128), F32),
         vmem((SECTIONS, 128), F32), vmem((DP, SECTIONS, 128), F32),
-        vmem((TOK, 128), F32), vmem((TOK, 128), F32),
+        vmem((TOK, 128), F32), vmem((SECTIONS, TOK, 128), F32),
         vmem((3 * IN, OUT), BF16),
-        vmem((DP * TOK, 3 * IN), BF16),
+        vmem((DP * TOK, 3 * IN), BF16), vmem((3 * IN, DP * TOK), BF16),
         vmem((DP, TOK, OUT), BF16), vmem((4, TOK, HALF), F32), vmem((2, TOK, HALF), F32),
         vmem((4, TOK, HALF), BF16), vmem((DP, TOK, HALF), BF16),
         vmem((4, TOK, HALF), BF16), vmem((4, TOK, HALF), BF16),
@@ -512,11 +567,10 @@
         vmem((STEPS, 8, 128), F32), vmem((8, 128), F32), vmem((SEG, 8, 128), F32),
         vmem((DP * TOK, OUT), BF16),
         dma((10,)), dma((5,)), dma((SEG,)), dma((10,)), dma((DP,)), dma((4,)),
-        dma((SEG,)), dma((SEG,)), dma((DP,)), dma((DP,)), dma((4,)), dma((4,)),
+        dma((SEG,)), dma((SEG,)), dma((DP,)), dma((DP,)), dma((DP,)), dma((DP,)),
         dma((4,)), dma((4,)), dma((DP,)), dma((DP,)), dma((4,)), dma((4,)), dma((1,)), dma((1,)),
-        dma((8,)), dma((2 * DP,)), dma((3,)), dma((4,)), dma((3,)), dma((4,)), dma((SEG,)), dma((SEG,)),
+        dma((8,)), dma((2 * DP,)), dma((3,)), dma((4,)), dma((3,)), dma((4,)), dma((SEG,)), dma((SEG,)), dma((6,)),
     ]
-    any_space = pl.BlockSpec(memory_space=pl.ANY)
     in_hbm = pl.BlockSpec(memory_space=pltpu.HBM)
     in_vmem = pl.BlockSpec(memory_space=pltpu.VMEM)
     loss, feat_t, rows = pl.pallas_call(
@@ -527,7 +581,7 @@
             jax.ShapeDtypeStruct((DP * TOK, OUT), BF16),
         ),
         in_specs=[in_hbm] * 7,
-        out_specs=(in_vmem, in_vmem, any_space),
+        out_specs=(in_vmem, in_hbm, in_hbm),
         scratch_shapes=scratch,
         compiler_params=pltpu.CompilerParams(
             collective_id=0, has_side_effects=True, vmem_limit_bytes=VM1 * 1024 * 1024
@@ -540,9 +594,12 @@
             jax.ShapeDtypeStruct((3 * IN, OUT), F32),
             jax.ShapeDtypeStruct((1, STEPS), F32),
         ),
-        in_specs=[in_vmem] * 3,
-        out_specs=(any_space, in_vmem),
-        scratch_shapes=[vmem((12, 256, OUT), F32), dma((12,))],
+        in_specs=[in_hbm] * 3,
+        out_specs=(in_hbm, in_vmem),
+        scratch_shapes=[
+            vmem((3 * IN, DP * TOK), BF16), vmem((DP * TOK, OUT), BF16), vmem((8, 128), F32),
+            vmem((6, 512, OUT), F32), dma((8,)), dma((6,)),
+        ],
         compiler_params=pltpu.CompilerParams(vmem_limit_bytes=VM2 * 1024 * 1024),
         name="gradient",
     )(feat_t, rows, loss)

time: 92.6 us -> 79.6 us (0.86); the launches traced: 91.2 us -> 79.5 us
  local copies, waits for them, and re-layouts: 7.01 us -> 0 us
  Pallas kernels: 83.6 us -> 78.8 us
    unnamed x14 -> x0, local copies, waits for them, and re-layouts: 7.01 us -> none
    pallas_call x1, Pallas kernels: 76.9 us -> 71.5 us  [local(): pl.pallas_call(kernel, out_shape=(jax.ShapeDtypeStruct((8, 128), F32), ja...]
where the time goes in v4:
time: 79.6 us; the launch traced here: 79.5 us
  Pallas kernels  78.8 us (99%)
    pallas_call x1, Pallas kernels, local(): pl.pallas_call(kernel, out_shape=(jax.ShapeDtypeStruct((8, 128), F32), ja...  71.5 us
    pallas_call x1, Pallas kernels, local(): pl.pallas_call(gradient, out_shape=(jax.ShapeDtypeStruct((3 * IN, OUT), F...  7.4 us

profile of v4, /device:TPU:1, one launch (start us, length us, event | category | flops | bytes accessed | tf_op | source)
XLA Modules:
  0.0 79.5 jit_solution(14633982442816206492)
XLA Ops:
  0.6 71.5 %window.1 = (f32[8,128]{1,0:T(8,128)}, bf16[3072,1024]{1,0:T(8,128)(2,1)}, bf16[1024,512]{1,0:T(8,128)(2,1)}) custom-call(bf16[128,8192]{1,0:T(8,128)(2,1)} %stream.1, f32[1,8192]{1,0:T(1,128)} %gain.1, f32[1,8192]{1,0:T(1,128)} %mix.1, bf16[3,1024,512]{2,1,0:T(8,128)(2,1)} %weight.1, f32[1,512]{1,0:T(1,128)} %bitcast.2, s32[1,8]{1,0:T(1,128)} %lengths_in.1, ...), custom_call_target="tpu_custom_call" | custom-call | tf_op jit(solution)/shard_map/window/pallas_call | solution.py:576
  72.1 7.4 %gradient.1 = (f32[3072,512]{1,0:T(8,128)}, f32[1,7]{1,0:T(1,128)}) custom-call(bf16[3072,1024]{1,0:T(8,128)(2,1)} %get-tuple-element.7.feat_in, bf16[1024,512]{1,0:T(8,128)(2,1)} %get-tuple-element.8.rows_in, f32[8,128]{1,0:T(8,128)} %get-tuple-element.9.loss_in), custom_call_target="tpu_custom_call" | custom-call | tf_op jit(solution)/shard_map/gradient/pallas_call | solution.py:591

commit v5 on v4

--- a/solution.py
+++ b/solution.py
@@ -16,8 +16,9 @@
 TOK = 128
 SEG = 16
 DP = 8
-VM1 = 56
-VM2 = 56
+CHUNK = 768
+VM1 = 47
+VM2 = 46
 IN = D // DP
 OUT = D // SEG
 OWN = TOK // SEG
@@ -49,13 +50,13 @@
     return taps
 
 
-def kernel(stream, gain, mix, weight, decay_in, lengths_in, mask_in, loss_out, feat_out, rows_out,
+def kernel(stream, gain, mix, weight, decay_in, lengths_in, mask_in, loss_out, feat_t, rows_out,
            decay, lengths, mask, params, gain_b, mix_b, gain_u, mix_u, rows16, hx, h0, tile, sc1, packed, sc2, inv_own, inv_b,
-           w, feat, feat_t, stage, keep_a, keep_b, in_a1, in_b1, out_a2, in_a2, out_b2, in_b2, own,
+           w, feat, stage, keep_a, keep_b, in_a1, in_b1, out_a2, in_a2, out_b2, in_b2, own,
            up_in, upper, mask_t, mask_pad, left, loss_acc, loss_tile, loss_all, rows_all,
            in_sem, g_send, g_recv, gf_send, h_send, h_recv, r1_send, r1_recv, r2_send, r2_recv, f_send, f_recv,
            a1_send, a1_recv, b1_send, b1_recv, a2_send, a2_recv, b2_send, b2_recv,
-           q_send, q_recv, qa_send, qa_recv, qb_send, qb_recv, l_send, l_recv, o_sem):
+           q_send, q_recv, qa_send, qa_recv, qb_send, qb_recv, l_send, l_recv):
     s = lax.axis_index("segment")
     d = lax.axis_index("dp")
     c = lax.rem(s, 2)
@@ -94,13 +95,13 @@
         copy.start()
 
     barrier = pltpu.get_barrier_semaphore()
-    for peer in seg_peers:
+    for peer in [across, sib] + x_peers:
         pl.semaphore_signal(barrier, inc=1, device_id=at(peer, d), device_id_type=MESH)
     for seg, peer in far + [(s, pair)]:
         pl.semaphore_signal(barrier, inc=1, device_id=at(seg, peer), device_id_type=MESH)
     gain_copy.wait()
     mix_copy.wait()
-    pl.semaphore_wait(barrier, SEG - 1 + DP)
+    pl.semaphore_wait(barrier, 5 + DP)
 
     def g_copy(slot, peer, send):
         return remote(params.at[slot], params.at[slot], send, g_recv.at[slot], device_id=at(peer, d))
@@ -337,10 +338,6 @@
 
     pl.when(home)(find_upper)
 
-    def turn_out(t):
-        rows = pl.ds(pl.multiple_of(t * 512, 512), 512)
-        return pltpu.make_async_copy(feat_t.at[rows], feat_out.at[rows], o_sem.at[t])
-
     def turn(t, _):
         cols = pl.ds(pl.multiple_of(t * 512, 512), 512)
 
@@ -350,7 +347,6 @@
             return 0
 
         lax.fori_loop(0, 8, block, 0)
-        turn_out(t).start()
         return 0
 
     @pl.when(jnp.logical_not(home))
@@ -442,21 +438,23 @@
         block = rows_all.at[rows_of(from_y * 2 + z), second]
         return remote(block, block, qb_send.at[i], qb_recv.at[from_y], device_id=at(s, pair))
 
+    b2_copy().wait_recv()
+    own[:, HALF:OUT] += in_b2[...].astype(F32)
+    lax.fori_loop(2, 4, draft, 0)
+    over_y = [p * 2 + zh for p in y_peers]
+    for i, peer in enumerate(over_y):
+        post(q_copy(1, 1 + i, d, peer))
     for i, from_y in enumerate(y_peers):
         remote(
             out_a2.at[0], in_a2.at[from_y], a2_send.at[0], a2_recv.at[from_y], device_id=at(s, from_y * 2 + zh)
         ).wait_recv()
         own[:, 0:HALF] += in_a2[from_y].astype(F32)
     lax.fori_loop(0, 2, draft, 0)
-    for i, peer in enumerate([pair] + [p * 2 + zh for p in y_peers]):
-        post(q_copy(0, i, d, peer))
-    b2_copy().wait_recv()
-    own[:, HALF:OUT] += in_b2[...].astype(F32)
-    lax.fori_loop(2, 4, draft, 0)
-    for i, peer in enumerate([pair] + [p * 2 + zh for p in y_peers]):
-        post(q_copy(1, i, d, peer))
-
+    post(q_copy(0, 0, d, pair))
     lax.fori_loop(4, 5, turn, 0)
+    for i, peer in enumerate(over_y):
+        post(q_copy(0, 1 + i, d, peer))
+    post(q_copy(1, 0, d, pair))
     q_copy(0, 0, pair, pair).wait_recv()
     for i, to_y in enumerate(y_peers):
         post(qa_copy(i, y, to_y))
@@ -507,39 +505,22 @@
     for to_y in y_peers:
         for z in range(2):
             b1_copy(to_y, z).wait_send()
-    for t in range(6):
-        turn_out(t).wait()
     rows_copy.wait()
 
 
-def gradient(feat_in, rows_in, loss_in, grad_out, loss_out, feat_t, rows, loss, grad, i_sem, sem):
-    def block(t):
-        return pl.ds(pl.multiple_of(t * 512, 512), 512)
-
-    def in_copy(t):
-        return pltpu.make_async_copy(feat_in.at[block(t)], feat_t.at[block(t)], i_sem.at[t])
-
+def gradient(feat_t, rows, loss, grad_out, loss_out, grad, sem):
     def out_copy(t):
-        return pltpu.make_async_copy(grad.at[t], grad_out.at[block(t)], sem.at[t])
-
-    rows_copy = pltpu.make_async_copy(rows_in, rows, i_sem.at[6])
-    loss_copy = pltpu.make_async_copy(loss_in, loss, i_sem.at[7])
-    rows_copy.start()
-    for t in range(6):
-        in_copy(t).start()
-    loss_copy.start()
-    rows_copy.wait()
+        return pltpu.make_async_copy(grad.at[t], grad_out.at[pl.ds(pl.multiple_of(t * CHUNK, CHUNK), CHUNK)], sem.at[t])
 
     def one(t, _):
-        in_copy(t).wait()
-        grad[t] = jnp.dot(feat_t[block(t), :], rows[...], preferred_element_type=F32)
+        block = pl.ds(pl.multiple_of(t * CHUNK, CHUNK), CHUNK)
+        grad[t] = jnp.dot(feat_t[block, :], rows[...], preferred_element_type=F32)
         out_copy(t).start()
         return 0
 
-    lax.fori_loop(0, 6, one, 0)
-    loss_copy.wait()
+    lax.fori_loop(0, 3 * IN // CHUNK, one, 0)
     loss_out[...] = loss[0:1, 0:STEPS]
-    for t in range(6):
+    for t in range(3 * IN // CHUNK):
         out_copy(t).wait()
 
 
@@ -557,7 +538,7 @@
         vmem((SECTIONS, 128), F32), vmem((DP, SECTIONS, 128), F32),
         vmem((TOK, 128), F32), vmem((SECTIONS, TOK, 128), F32),
         vmem((3 * IN, OUT), BF16),
-        vmem((DP * TOK, 3 * IN), BF16), vmem((3 * IN, DP * TOK), BF16),
+        vmem((DP * TOK, 3 * IN), BF16),
         vmem((DP, TOK, OUT), BF16), vmem((4, TOK, HALF), F32), vmem((2, TOK, HALF), F32),
         vmem((4, TOK, HALF), BF16), vmem((DP, TOK, HALF), BF16),
         vmem((4, TOK, HALF), BF16), vmem((4, TOK, HALF), BF16),
@@ -569,19 +550,19 @@
         dma((10,)), dma((5,)), dma((SEG,)), dma((10,)), dma((DP,)), dma((4,)),
         dma((SEG,)), dma((SEG,)), dma((DP,)), dma((DP,)), dma((DP,)), dma((DP,)),
         dma((4,)), dma((4,)), dma((DP,)), dma((DP,)), dma((4,)), dma((4,)), dma((1,)), dma((1,)),
-        dma((8,)), dma((2 * DP,)), dma((3,)), dma((4,)), dma((3,)), dma((4,)), dma((SEG,)), dma((SEG,)), dma((6,)),
+        dma((8,)), dma((2 * DP,)), dma((3,)), dma((4,)), dma((3,)), dma((4,)), dma((SEG,)), dma((SEG,)),
     ]
     in_hbm = pl.BlockSpec(memory_space=pltpu.HBM)
     in_vmem = pl.BlockSpec(memory_space=pltpu.VMEM)
     loss, feat_t, rows = pl.pallas_call(
         kernel,
         out_shape=(
-            jax.ShapeDtypeStruct((8, 128), F32),
-            jax.ShapeDtypeStruct((3 * IN, DP * TOK), BF16),
-            jax.ShapeDtypeStruct((DP * TOK, OUT), BF16),
+            vmem((8, 128), F32),
+            vmem((3 * IN, DP * TOK), BF16),
+            vmem((DP * TOK, OUT), BF16),
         ),
         in_specs=[in_hbm] * 7,
-        out_specs=(in_vmem, in_hbm, in_hbm),
+        out_specs=(in_vmem, in_vmem, in_vmem),
         scratch_shapes=scratch,
         compiler_params=pltpu.CompilerParams(
             collective_id=0, has_side_effects=True, vmem_limit_bytes=VM1 * 1024 * 1024
@@ -594,12 +575,9 @@
             jax.ShapeDtypeStruct((3 * IN, OUT), F32),
             jax.ShapeDtypeStruct((1, STEPS), F32),
         ),
-        in_specs=[in_hbm] * 3,
+        in_specs=[in_vmem] * 3,
         out_specs=(in_hbm, in_vmem),
-        scratch_shapes=[
-            vmem((3 * IN, DP * TOK), BF16), vmem((DP * TOK, OUT), BF16), vmem((8, 128), F32),
-            vmem((6, 512, OUT), F32), dma((8,)), dma((6,)),
-        ],
+        scratch_shapes=[vmem((3 * IN // CHUNK, CHUNK, OUT), F32), dma((3 * IN // CHUNK,))],
         compiler_params=pltpu.CompilerParams(vmem_limit_bytes=VM2 * 1024 * 1024),
         name="gradient",
     )(feat_t, rows, loss)

time: 79.6 us -> 74.8 us (0.940)
  Pallas kernels: 78.8 us -> 74 us
    pallas_call x1, Pallas kernels: 71.5 us -> 68.4 us  [local(): pl.pallas_call(kernel, out_shape=(vmem((8, 128), F32), vmem((3 * IN, DP *...]
    pallas_call x1, Pallas kernels: 7.4 us -> 5.6 us  [local(): pl.pallas_call(gradient, out_shape=(jax.ShapeDtypeStruct((3 * IN, OUT), F...]
where the time goes in v5:
time: 74.8 us; the launch traced here: 74.6 us
  Pallas kernels  74 us (99%)
    pallas_call x1, Pallas kernels, local(): pl.pallas_call(kernel, out_shape=(vmem((8, 128), F32), vmem((3 * IN, DP *...  68.4 us
    pallas_call x1, Pallas kernels, local(): pl.pallas_call(gradient, out_shape=(jax.ShapeDtypeStruct((3 * IN, OUT), F...  5.6 us

profile of v5, /device:TPU:1, one launch (start us, length us, event | category | flops | bytes accessed | tf_op | source)
XLA Modules:
  0.0 74.6 jit_solution(16944401283197063831)
XLA Ops:
  0.6 68.4 %window.1 = (f32[8,128]{1,0:T(8,128)S(1)}, bf16[3072,1024]{1,0:T(8,128)(2,1)S(1)}, bf16[1024,512]{1,0:T(8,128)(2,1)S(1)}) custom-call(bf16[128,8192]{1,0:T(8,128)(2,1)} %stream.1, f32[1,8192]{1,0:T(1,128)} %gain.1, f32[1,8192]{1,0:T(1,128)} %mix.1, bf16[3,1024,512]{2,1,0:T(8,128)(2,1)} %weight.1, f32[1,512]{1,0:T(1,128)} %bitcast.2, s32[1,8]{1,0:T(1,128)} %lengths_in.1, ...), custom_call_target="tpu_custom_call" | custom-call | tf_op jit(solution)/shard_map/window/pallas_call | solution.py:557
  69.0 5.6 %gradient.1 = (f32[3072,512]{1,0:T(8,128)}, f32[1,7]{1,0:T(1,128)}) custom-call(bf16[3072,1024]{1,0:T(8,128)(2,1)S(1)} %get-tuple-element.7.feat_t, bf16[1024,512]{1,0:T(8,128)(2,1)S(1)} %get-tuple-element.8.rows, f32[8,128]{1,0:T(8,128)S(1)} %get-tuple-element.9.loss), custom_call_target="tpu_custom_call" | custom-call | tf_op jit(solution)/shard_map/gradient/pallas_call | solution.py:572

commit v6 on v5

--- a/solution.py
+++ b/solution.py
@@ -50,10 +50,10 @@
     return taps
 
 
-def kernel(stream, gain, mix, weight, decay_in, lengths_in, mask_in, loss_out, feat_t, rows_out,
+def kernel(stream, gain, mix, weight, decay_in, lengths_in, mask_in, loss_out, feat_t, rows_all,
            decay, lengths, mask, params, gain_b, mix_b, gain_u, mix_u, rows16, hx, h0, tile, sc1, packed, sc2, inv_own, inv_b,
            w, feat, stage, keep_a, keep_b, in_a1, in_b1, out_a2, in_a2, out_b2, in_b2, own,
-           up_in, upper, mask_t, mask_pad, left, loss_acc, loss_tile, loss_all, rows_all,
+           up_in, upper, mask_t, mask_pad, left, loss_acc, loss_tile, loss_all,
            in_sem, g_send, g_recv, gf_send, h_send, h_recv, r1_send, r1_recv, r2_send, r2_recv, f_send, f_recv,
            a1_send, a1_recv, b1_send, b1_recv, a2_send, a2_recv, b2_send, b2_recv,
            q_send, q_recv, qa_send, qa_recv, qb_send, qb_recv, l_send, l_recv):
@@ -100,6 +100,7 @@
     for seg, peer in far + [(s, pair)]:
         pl.semaphore_signal(barrier, inc=1, device_id=at(seg, peer), device_id_type=MESH)
     gain_copy.wait()
+    params[s, 0] = 0.5 * params[s, 0]
     mix_copy.wait()
     pl.semaphore_wait(barrier, 5 + DP)
 
@@ -176,12 +177,12 @@
     def scale_step(sec, carry):
         inv, acc = carry
         acc = jnp.where(lane == sec, inv, acc)
-        h = advance(hx[half, :], 0.5 * params[sec, 0], params[sec, 1], inv).astype(F32)
+        h = advance(hx[half, :], params[sec, 0], params[sec, 1], inv).astype(F32)
         hx[half, :] = h
         return inverse(h), acc
 
     inv, acc = lax.fori_loop(
-        0, SECTIONS - 1, scale_step, (inverse(hx[half, :]), jnp.zeros((OWN, 128), F32))
+        0, SECTIONS - 1, scale_step, (inverse(hx[half, :]), jnp.zeros((OWN, 128), F32)), unroll=5
     )
     tile[...] = jnp.where(lane == SECTIONS - 1, inv, acc)
     sc1[s] = tile[...]
@@ -192,9 +193,9 @@
     def spread(sec, _):
         mine = pl.ds(pl.multiple_of(d * IN, IN), IN)
         loss_cols = pl.ds(pl.multiple_of(s * OUT, OUT), OUT)
-        gain_b[sec] = jnp.broadcast_to(0.5 * params[sec, 0, :, mine], (8, IN))
+        gain_b[sec] = jnp.broadcast_to(params[sec, 0, :, mine], (8, IN))
         mix_b[sec] = jnp.broadcast_to(params[sec, 1, :, mine], (8, IN))
-        gain_u[sec] = jnp.broadcast_to(0.5 * params[sec, 0, :, loss_cols], (8, OUT))
+        gain_u[sec] = jnp.broadcast_to(params[sec, 0, :, loss_cols], (8, OUT))
         mix_u[sec] = jnp.broadcast_to(params[sec, 1, :, loss_cols], (8, OUT))
         return 0
 
@@ -265,10 +266,8 @@
     def b2_copy():
         return remote(out_b2, in_b2, b2_send.at[0], b2_recv.at[0], device_id=at(s, pair))
 
-    def join(j, z):
+    def give(j, z, part):
         to_y = j // 2
-        rows = pl.ds(pl.multiple_of(j * TOK, TOK), TOK)
-        part = jnp.dot(feat[rows, :], w[...], preferred_element_type=F32)
         stage[j] = part.astype(BF16)
 
         @pl.when(z == zh)
@@ -292,11 +291,14 @@
         slot = (j // 2) * 2 + part
         return remote(feat.at[rows], feat.at[rows], f_send.at[slot], f_recv.at[slot], device_id=at(sib, d))
 
-    def join_other(n):
-        j = replica_of(1 - c, n)
-        f_copy(j, 0).wait_recv()
-        f_copy(j, 1).wait_recv()
-        join(j, 1 - c)
+    def join(n):
+        to_y = lax.rem(y + n, 4)
+        for part in range(2):
+            f_copy(to_y * 2 + 1 - c, part).wait_recv()
+        rows = pl.ds(pl.multiple_of(to_y * 2 * TOK, 2 * TOK), 2 * TOK)
+        both = jnp.dot(feat[rows, :], w[...], preferred_element_type=F32)
+        for z in range(2):
+            give(to_y * 2 + z, z, both[z * TOK:(z + 1) * TOK, :])
 
     def work(n, _):
         j = replica_of(c, n)
@@ -325,16 +327,25 @@
         f_copy(j, 0).start()
         lax.fori_loop(4, 8, one, 0)
         f_copy(j, 1).start()
-        join(j, c)
 
         @pl.when(n > 0)
         def _():
-            join_other(n - 1)
+            join(n - 1)
 
         return 0
 
     lax.fori_loop(0, 4, work, 0)
-    join_other(3)
+
+    last = lax.rem(y + 3, 4) * 2
+
+    def last_one(z):
+        j = last + z
+        give(j, z, jnp.dot(feat[pl.ds(pl.multiple_of(j * TOK, TOK), TOK), :], w[...], preferred_element_type=F32))
+
+    last_one(c)
+    for part in range(2):
+        f_copy(last + 1 - c, part).wait_recv()
+    last_one(1 - c)
 
     pl.when(home)(find_upper)
 
@@ -438,6 +449,7 @@
         block = rows_all.at[rows_of(from_y * 2 + z), second]
         return remote(block, block, qb_send.at[i], qb_recv.at[from_y], device_id=at(s, pair))
 
+    early, sends[:] = list(sends), []
     b2_copy().wait_recv()
     own[:, HALF:OUT] += in_b2[...].astype(F32)
     lax.fori_loop(2, 4, draft, 0)
@@ -460,6 +472,24 @@
         post(qa_copy(i, y, to_y))
 
     lax.fori_loop(5, 6, turn, 0)
+    for copy in early:
+        copy.wait_send()
+
+    @pl.when(home)
+    def _():
+        for i in range(DP - 1):
+            h_copy(i).wait_send()
+            r2_copy(i).wait_send()
+
+    for n in range(4):
+        for part in range(2):
+            f_copy(replica_of(c, n), part).wait_send()
+    for to_y in range(4):
+        a1_copy(to_y).wait_send()
+    for to_y in y_peers:
+        for z in range(2):
+            b1_copy(to_y, z).wait_send()
+
     for i, from_y in enumerate(y_peers):
         q_copy(1, 0, from_y * 2 + zh, pair).wait_recv()
         post(qb_copy(i, from_y, zh))
@@ -485,27 +515,9 @@
         q_copy(0, 0, from_y * 2 + zh, pair).wait_recv()
         qa_copy(0, from_y, from_y).wait_recv()
         qb_copy(0, from_y, 1 - zh).wait_recv()
-    rows_copy = pltpu.make_async_copy(rows_all, rows_out, in_sem.at[0])
-    rows_copy.start()
 
     for copy in sends:
         copy.wait_send()
-
-    @pl.when(home)
-    def _():
-        for i in range(DP - 1):
-            h_copy(i).wait_send()
-            r2_copy(i).wait_send()
-
-    for n in range(4):
-        for part in range(2):
-            f_copy(replica_of(c, n), part).wait_send()
-    for to_y in range(4):
-        a1_copy(to_y).wait_send()
-    for to_y in y_peers:
-        for z in range(2):
-            b1_copy(to_y, z).wait_send()
-    rows_copy.wait()
 
 
 def gradient(feat_t, rows, loss, grad_out, loss_out, grad, sem):
@@ -546,7 +558,6 @@
         vmem((TOK, OUT), BF16), vmem((TOK, OUT), F32),
         vmem((TOK, 128), F32), vmem((TOK, 128), F32), vmem((TOK, 128), jnp.int32),
         vmem((STEPS, 8, 128), F32), vmem((8, 128), F32), vmem((SEG, 8, 128), F32),
-        vmem((DP * TOK, OUT), BF16),
         dma((10,)), dma((5,)), dma((SEG,)), dma((10,)), dma((DP,)), dma((4,)),
         dma((SEG,)), dma((SEG,)), dma((DP,)), dma((DP,)), dma((DP,)), dma((DP,)),
         dma((4,)), dma((4,)), dma((DP,)), dma((DP,)), dma((4,)), dma((4,)), dma((1,)), dma((1,)),

time: 74.8 us -> 72.6 us (0.971)
  Pallas kernels: 74 us -> 71.9 us
    pallas_call x1, Pallas kernels: 68.4 us -> 66.3 us  [local(): pl.pallas_call(kernel, out_shape=(vmem((8, 128), F32), vmem((3 * IN, DP *...]
where the time goes in v6:
time: 72.6 us; the launch traced here: 72.5 us
  Pallas kernels  71.9 us (99%)
    pallas_call x1, Pallas kernels, local(): pl.pallas_call(kernel, out_shape=(vmem((8, 128), F32), vmem((3 * IN, DP *...  66.3 us
    pallas_call x1, Pallas kernels, local(): pl.pallas_call(gradient, out_shape=(jax.ShapeDtypeStruct((3 * IN, OUT), F...  5.6 us

profile of v6, /device:TPU:1, one launch (start us, length us, event | category | flops | bytes accessed | tf_op | source)
XLA Modules:
  0.0 72.5 jit_solution(9990809429027597070)
XLA Ops:
  0.6 66.3 %window.1 = (f32[8,128]{1,0:T(8,128)S(1)}, bf16[3072,1024]{1,0:T(8,128)(2,1)S(1)}, bf16[1024,512]{1,0:T(8,128)(2,1)S(1)}) custom-call(bf16[128,8192]{1,0:T(8,128)(2,1)} %stream.1, f32[1,8192]{1,0:T(1,128)} %gain.1, f32[1,8192]{1,0:T(1,128)} %mix.1, bf16[3,1024,512]{2,1,0:T(8,128)(2,1)} %weight.1, f32[1,512]{1,0:T(1,128)} %bitcast.2, s32[1,8]{1,0:T(1,128)} %lengths_in.1, ...), custom_call_target="tpu_custom_call" | custom-call | tf_op jit(solution)/shard_map/window/pallas_call | solution.py:568
  66.9 5.6 %gradient.1 = (f32[3072,512]{1,0:T(8,128)}, f32[1,7]{1,0:T(1,128)}) custom-call(bf16[3072,1024]{1,0:T(8,128)(2,1)S(1)} %get-tuple-element.7.feat_t, bf16[1024,512]{1,0:T(8,128)(2,1)S(1)} %get-tuple-element.8.rows, f32[8,128]{1,0:T(8,128)S(1)} %get-tuple-element.9.loss), custom_call_target="tpu_custom_call" | custom-call | tf_op jit(solution)/shard_map/gradient/pallas_call | solution.py:583

commit v7 on v6

--- a/solution.py
+++ b/solution.py
@@ -16,7 +16,7 @@
 TOK = 128
 SEG = 16
 DP = 8
-CHUNK = 768
+CHUNK = 1024
 VM1 = 47
 VM2 = 46
 IN = D // DP
@@ -396,7 +396,7 @@
     def _():
         lax.fori_loop(0, 2, turn, 0)
 
-    lax.fori_loop(2, 4, turn, 0)
+    lax.fori_loop(2, 3, turn, 0)
 
     inv_count = []
     for k in range(1, STEPS + 1):
@@ -463,13 +463,27 @@
         own[:, 0:HALF] += in_a2[from_y].astype(F32)
     lax.fori_loop(0, 2, draft, 0)
     post(q_copy(0, 0, d, pair))
-    lax.fori_loop(4, 5, turn, 0)
+    lax.fori_loop(3, 4, turn, 0)
     for i, peer in enumerate(over_y):
         post(q_copy(0, 1 + i, d, peer))
     post(q_copy(1, 0, d, pair))
     q_copy(0, 0, pair, pair).wait_recv()
     for i, to_y in enumerate(y_peers):
         post(qa_copy(i, y, to_y))
+
+    lax.fori_loop(4, 5, turn, 0)
+    for i, from_y in enumerate(y_peers):
+        q_copy(1, 0, from_y * 2 + zh, pair).wait_recv()
+        post(qb_copy(i, from_y, zh))
+
+    lane = lax.broadcasted_iota(jnp.int32, (8, 128), 1)
+    losses = jnp.zeros((8, 128), F32)
+    for k in range(1, STEPS + 1):
+        losses = jnp.where(lane == k - 1, jnp.sum(loss_acc[k - 1]) * inv_count[k - 1], losses)
+    loss_tile[...] = losses
+    loss_all[s] = losses
+    for i, peer in enumerate(seg_peers):
+        post(remote(loss_tile, loss_all.at[s], l_send.at[i], l_recv.at[s], device_id=at(peer, d)))
 
     lax.fori_loop(5, 6, turn, 0)
     for copy in early:
@@ -489,19 +503,6 @@
     for to_y in y_peers:
         for z in range(2):
             b1_copy(to_y, z).wait_send()
-
-    for i, from_y in enumerate(y_peers):
-        q_copy(1, 0, from_y * 2 + zh, pair).wait_recv()
-        post(qb_copy(i, from_y, zh))
-
-    lane = lax.broadcasted_iota(jnp.int32, (8, 128), 1)
-    losses = jnp.zeros((8, 128), F32)
-    for k in range(1, STEPS + 1):
-        losses = jnp.where(lane == k - 1, jnp.sum(loss_acc[k - 1]) * inv_count[k - 1], losses)
-    loss_tile[...] = losses
-    loss_all[s] = losses
-    for i, peer in enumerate(seg_peers):
-        post(remote(loss_tile, loss_all.at[s], l_send.at[i], l_recv.at[s], device_id=at(peer, d)))
 
     for i, peer in enumerate(seg_peers):
         remote(loss_tile, loss_all.at[peer], l_send.at[i], l_recv.at[peer], device_id=at(peer, d)).wait_recv()

time: 72.6 us -> 72.6 us (level)
  no operation moved by 1% of the time
where the time goes in v7:
time: 72.6 us; the launch traced here: 72.5 us
  Pallas kernels  71.8 us (99%)
    pallas_call x1, Pallas kernels, local(): pl.pallas_call(kernel, out_shape=(vmem((8, 128), F32), vmem((3 * IN, DP *...  66.2 us
    pallas_call x1, Pallas kernels, local(): pl.pallas_call(gradient, out_shape=(jax.ShapeDtypeStruct((3 * IN, OUT), F...  5.59 us

profile of v7, /device:TPU:1, one launch (start us, length us, event | category | flops | bytes accessed | tf_op | source)
XLA Modules:
  0.0 72.5 jit_solution(2291549061371692826)
XLA Ops:
  0.6 66.2 %window.1 = (f32[8,128]{1,0:T(8,128)S(1)}, bf16[3072,1024]{1,0:T(8,128)(2,1)S(1)}, bf16[1024,512]{1,0:T(8,128)(2,1)S(1)}) custom-call(bf16[128,8192]{1,0:T(8,128)(2,1)} %stream.1, f32[1,8192]{1,0:T(1,128)} %gain.1, f32[1,8192]{1,0:T(1,128)} %mix.1, bf16[3,1024,512]{2,1,0:T(8,128)(2,1)} %weight.1, f32[1,512]{1,0:T(1,128)} %bitcast.2, s32[1,8]{1,0:T(1,128)} %lengths_in.1, ...), custom_call_target="tpu_custom_call" | custom-call | tf_op jit(solution)/shard_map/window/pallas_call | solution.py:569
  66.9 5.6 %gradient.1 = (f32[3072,512]{1,0:T(8,128)}, f32[1,7]{1,0:T(1,128)}) custom-call(bf16[3072,1024]{1,0:T(8,128)(2,1)S(1)} %get-tuple-element.7.feat_t, bf16[1024,512]{1,0:T(8,128)(2,1)S(1)} %get-tuple-element.8.rows, f32[8,128]{1,0:T(8,128)S(1)} %get-tuple-element.9.loss), custom_call_target="tpu_custom_call" | custom-call | tf_op jit(solution)/shard_map/gradient/pallas_call | solution.py:584

commit v8 on v7

--- a/solution.py
+++ b/solution.py
@@ -186,7 +186,7 @@
     )
     tile[...] = jnp.where(lane == SECTIONS - 1, inv, acc)
     sc1[s] = tile[...]
-    chips = [lax.rem(s // 2 + i, SEG // 2) * 2 for i in range(1, SEG // 2)]
+    chips = [lax.rem(s // 2 + i, SEG // 2) * 2 for i in (6, 2, 5, 7, 3, 1, 4)]
     for i, peer in enumerate([p + zh for p in chips] + [sib] + [p + 1 - zh for p in chips]):
         post(remote(tile, sc1.at[s], r1_send.at[i], r1_recv.at[s], device_id=at(peer, d)))
 

time: 72.6 us -> 72.5 us (level)
  no operation moved by 1% of the time
where the time goes in v8:
time: 72.5 us; the launch traced here: 72.4 us
  Pallas kernels  71.7 us (99%)
    pallas_call x1, Pallas kernels, local(): pl.pallas_call(kernel, out_shape=(vmem((8, 128), F32), vmem((3 * IN, DP *...  66.2 us
    pallas_call x1, Pallas kernels, local(): pl.pallas_call(gradient, out_shape=(jax.ShapeDtypeStruct((3 * IN, OUT), F...  5.59 us

profile of v8, /device:TPU:1, one launch (start us, length us, event | category | flops | bytes accessed | tf_op | source)
XLA Modules:
  0.0 72.4 jit_solution(401068195170599157)
XLA Ops:
  0.6 66.2 %window.1 = (f32[8,128]{1,0:T(8,128)S(1)}, bf16[3072,1024]{1,0:T(8,128)(2,1)S(1)}, bf16[1024,512]{1,0:T(8,128)(2,1)S(1)}) custom-call(bf16[128,8192]{1,0:T(8,128)(2,1)} %stream.1, f32[1,8192]{1,0:T(1,128)} %gain.1, f32[1,8192]{1,0:T(1,128)} %mix.1, bf16[3,1024,512]{2,1,0:T(8,128)(2,1)} %weight.1, f32[1,512]{1,0:T(1,128)} %bitcast.2, s32[1,8]{1,0:T(1,128)} %lengths_in.1, ...), custom_call_target="tpu_custom_call" | custom-call | tf_op jit(solution)/shard_map/window/pallas_call | solution.py:569
  66.8 5.6 %gradient.1 = (f32[3072,512]{1,0:T(8,128)}, f32[1,7]{1,0:T(1,128)}) custom-call(bf16[3072,1024]{1,0:T(8,128)(2,1)S(1)} %get-tuple-element.7.feat_t, bf16[1024,512]{1,0:T(8,128)(2,1)S(1)} %get-tuple-element.8.rows, f32[8,128]{1,0:T(8,128)S(1)} %get-tuple-element.9.loss), custom_call_target="tpu_custom_call" | custom-call | tf_op jit(solution)/shard_map/gradient/pallas_call | solution.py:584
